TPU v7x, 256 devices: a whole 4x4x8 slice. The times are simulated.
256 devices in a mesh: gx: 16 (over z, core), gy: 4 (over x), gz: 4 (over y).
Axes of the slice: x: 4, y: 4, z: 8, core: 2. Of those that a mesh axis runs over, the one named last changes fastest.
Arguments:
- velocity: float32 [3, 256, 192, 512], P(None, 'gx', 'gz', 'gy'), may hold values from 0.5 to 1.5
- pressure: float32 [256, 192, 512], P('gx', 'gz', 'gy'), may hold values from -3 to 3
- kernel: float32 [65536, 128], P(('gx', 'gy', 'gz')), may hold values from 0.1 to 1
- owners: int32 [65536, 1], P(('gx', 'gy', 'gz')), may hold values from 0 to 63; in each aligned block of 256 rows (0 to 255, 256 to 511, ...) at most 8 rows name the same one
- lines: int32 [65536], P(('gx', 'gy', 'gz')), may hold values from 0 to 767
- point_turbine: int32 [65536], P(('gx', 'gy', 'gz')), may hold values from 0 to 47
- row_counts: int32 [16, 4, 4], P('gx', 'gy', 'gz'), may hold values from 128 to 256
- thrust: float32 [48], replicated, may hold values from 0.4 to 1
- inflow_x: int32 [48], replicated, may hold values from 0 to 255
- inflow_y: int32 [48], replicated, may hold values from 0 to 480
Outputs:
- velocity_out: float32 [3, 256, 192, 512], P(None, 'gx', 'gz', 'gy')
- pressure_out: float32 [256, 192, 512], P('gx', 'gz', 'gy')
Inputs may be any that keep to these rules, and one draw needn't show every extreme that they name: `owners`: among the rows of one device no horizontal block is named by more than 8 rows, and in every draw some device names one block exactly 8 times.
All inputs are finite; a program needn't handle non-finite values.
Results may differ from a plain program's by a relative error of at most 0.00011.
Values sent between devices are 32-bit elements; how exact they have to be, the bound alone decides.
A program may use at most 64 MiB of HBM per device.

v0:
```python
import jax
import jax.numpy as jnp
from jax import lax
from jax.sharding import PartitionSpec as P

BAND = 32
STEPS = 2
SWEEPS = 8


def extended(cells, sides, width):
    for axis, dim in sides:
        count = lax.axis_size(axis)
        ends = count - 1
        head = lax.slice_in_dim(cells, 0, width, axis=dim)
        tail = lax.slice_in_dim(cells, cells.shape[dim] - width, cells.shape[dim], axis=dim)
        cells = jnp.concatenate(
            [
                lax.ppermute(tail, axis, [(i, (i + 1) % count) for i in range(ends)]),
                cells,
                lax.ppermute(head, axis, [((i + 1) % count, i) for i in range(ends)]),
            ],
            axis=dim,
        )
    return cells


def neighbours(padded):
    total = padded[..., 2:, 1:-1, 1:-1] + padded[..., :-2, 1:-1, 1:-1]
    total = total + padded[..., 1:-1, 2:, 1:-1] + padded[..., 1:-1, :-2, 1:-1]
    total = total + padded[..., 1:-1, 1:-1, 2:] + padded[..., 1:-1, 1:-1, :-2]
    return total


def pressure_faces(press):
    return extended(press, (("gx", 0), ("gy", 2), ("gz", 1)), 1)


def body(
    velocity, pressure, kernel, owners, lines, point_turbine, row_counts, thrust, inflow_x, inflow_y
):
    time_step = 0.4
    viscosity = 0.05
    cells_x = velocity.shape[1]
    cells_z = velocity.shape[2]
    cells_y = velocity.shape[3]
    row_total = kernel.shape[0]
    turbines = thrust.shape[0]
    peers_x = lax.axis_size("gx")
    peers_y = lax.axis_size("gy")
    peers = peers_x * peers_y
    capacity = 2 * row_total // peers
    depth_total = cells_z * lax.axis_size("gz")
    start_x = lax.axis_index("gx") * cells_x
    start_y = lax.axis_index("gy") * cells_y
    xplaces = start_x + jnp.arange(cells_x)
    yplaces = start_y + jnp.arange(cells_y)
    pick_x = (inflow_x[:, None] == xplaces[None, :]).astype(jnp.float32)
    band = (
        (yplaces[None, :] >= inflow_y[:, None]) & (yplaces[None, :] < inflow_y[:, None] + BAND)
    ).astype(jnp.float32)
    valid = (jnp.arange(row_total) < row_counts.reshape(())).astype(jnp.float32)
    pick_turbine = (point_turbine[:, None] == jnp.arange(turbines)[None, :]).astype(jnp.float32)
    target = owners[:, 0]
    landing = (target[:, None] == jnp.arange(peers)[None, :]).astype(jnp.int32)
    earlier = jnp.cumsum(landing, axis=0) - landing
    slot_index = jnp.sum(earlier * landing, axis=1)
    field = velocity
    press = pressure
    for repeat in range(STEPS):
        plane = jnp.dot(
            pick_x, field[0].reshape(cells_x, cells_z * cells_y), precision=lax.Precision.HIGHEST
        )
        partial_sum = jnp.sum(
            plane.reshape(turbines, cells_z, cells_y) * band[:, None, :], axis=(1, 2)
        )
        total = lax.psum(partial_sum, ("gx", "gy", "gz"))
        uref = total / (BAND * depth_total)
        magnitude = 0.5 * thrust * uref * jnp.abs(uref)
        row_force = jnp.dot(pick_turbine, magnitude, precision=lax.Precision.HIGHEST) * valid
        values = kernel * row_force[:, None]
        send_values = (
            jnp.zeros((peers, capacity, cells_y), jnp.float32).at[target, slot_index].set(values)
        )
        send_lines = jnp.zeros((peers, capacity), jnp.int32).at[target, slot_index].set(lines)
        got_values, got_lines = (
            lax.all_to_all(send_values, ("gx", "gy"), split_axis=0, concat_axis=0, tiled=True),
            lax.all_to_all(send_lines, ("gx", "gy"), split_axis=0, concat_axis=0, tiled=True),
        )
        force = jnp.zeros((cells_x * cells_z, cells_y), jnp.float32)
        force = force.at[got_lines.reshape(-1)].add(got_values.reshape(-1, cells_y))
        force = force.reshape(cells_x, cells_z, cells_y)
        forcing = jnp.stack([force, jnp.zeros_like(force), jnp.zeros_like(force)])
        padded = extended(field, (("gx", 1), ("gy", 3), ("gz", 2)), 1)
        laplace = neighbours(padded) - 6.0 * field
        star = field + time_step * (viscosity * laplace - forcing)
        spad = extended(star, (("gx", 1), ("gy", 3), ("gz", 2)), 1)
        source = 0.5 * (spad[0, 2:, 1:-1, 1:-1] - spad[0, :-2, 1:-1, 1:-1])
        source = source + 0.5 * (spad[1, 1:-1, 1:-1, 2:] - spad[1, 1:-1, 1:-1, :-2])
        source = source + 0.5 * (spad[2, 1:-1, 2:, 1:-1] - spad[2, 1:-1, :-2, 1:-1])
        for sweep_index in range(SWEEPS):
            press = (neighbours(pressure_faces(press)) - source) / 6.0
        ppad = pressure_faces(press)
        grad_x = 0.5 * (ppad[2:, 1:-1, 1:-1] - ppad[:-2, 1:-1, 1:-1])
        grad_y = 0.5 * (ppad[1:-1, 1:-1, 2:] - ppad[1:-1, 1:-1, :-2])
        grad_z = 0.5 * (ppad[1:-1, 2:, 1:-1] - ppad[1:-1, :-2, 1:-1])
        field = star - jnp.stack([grad_x, grad_y, grad_z])
    return (field, press)


def solution(mesh):
    placed = (
        P(None, "gx", "gz", "gy"),
        P("gx", "gz", "gy"),
        P(("gx", "gy", "gz"), None),
        P(("gx", "gy", "gz"), None),
        P(("gx", "gy", "gz")),
        P(("gx", "gy", "gz")),
        P("gx", "gy", "gz"),
        P(),
        P(),
        P(),
    )
    return jax.shard_map(
        body,
        mesh=mesh,
        in_specs=placed,
        out_specs=(P(None, "gx", "gz", "gy"), P("gx", "gz", "gy")),
        check_vma=False,
    )
```

profile of v0, /device:TPU:1, one launch (start us, length us, event | category | flops | bytes accessed | tf_op | source)
XLA Modules:
  0.0 958.4 jit_solution(13235673349705863126)
XLA Ops:
  2.0 5.1 collective-permute-start.6
  12.2 21.2 %scatter_fusion = s32[64,8]{0,1:T(8,128)S(1)} fusion(s32[64,8]{0,1:T(8,128)S(1)} %broadcast.167, s32[256]{0:T(256)S(1)} %bitcast.99, s32[256]{0:T(256)} %param.14), kind=kCustom, calls=%fused_computation | custom fusion | bytes 5120 | tf_op jit(solution)/shard_map/scatter | solution.py:85
  34.2 10.9 %all-to-all-start = ((s32[64,1,8]{2,1,0:T(1,128)}), s32[64,1,8]{2,1,0:T(1,128)S(1)}, u32[]{:S(2)}, u32[]{:S(2)}) async-start(s32[64,1,8]{2,1,0:T(1,128)} %copy.41), calls=%async_computation | async-start | bytes 65536 | tf_op jit(solution)/shard_map/all_to_all | solution.py:88
  52.4 78.5 %psum.14 = f32[48]{0:T(128)S(1)} all-reduce(f32[48]{0:T(128)S(1)} %fusion), channel_id=1, replica_groups=mesh['gx'=16,'gy'=4,'gz'=4] {'gx','gy','gz'}, use_global_device_ids=true, to_apply=%region_5.6 | all-reduce | flops 48 | bytes 384 | tf_op jit(solution)/shard_map/psum | solution.py:77
  132.0 27.4 %scatter_fusion.1 = f32[64,8,128]{2,1,0:T(8,128)} fusion(f32[64,8,128]{2,1,0:T(8,128)} %broadcast.175.clone, s32[256]{0:T(256)S(1)} %bitcast.100, f32[256,128]{1,0:T(8,128)S(1)} %broadcast_multiply_fusion.1), kind=kCustom, calls=%fused_computation.1 | custom fusion | bytes 395264 | tf_op jit(solution)/shard_map/scatter | solution.py:83
  159.4 7.2 all-to-all-start.1
  194.4 5.6 fusion.17
  200.0 5.8 collective-permute-start.13
  263.9 6.8 collective-permute-done.21
  296.4 6.6 collective-permute-done.27
  328.8 6.6 collective-permute-done.33
  344.8 5.2 collective-permute-start.37
  361.4 6.6 collective-permute-done.39
  392.4 6.6 collective-permute-done.45
  408.3 5.2 collective-permute-start.49
  424.9 6.6 collective-permute-done.51
  440.9 5.1 collective-permute-start.55
  457.4 6.6 collective-permute-done.57
  487.7 7.1 collective-permute-done.63
  515.2 75.6 %psum.15 = f32[48]{0:T(128)S(1)} all-reduce(f32[48]{0:T(128)S(1)} %fusion.1), channel_id=1, replica_groups=mesh['gx'=16,'gy'=4,'gz'=4] {'gx','gy','gz'}, use_global_device_ids=true, to_apply=%region_9.10 | all-reduce | flops 48 | bytes 384 | tf_op jit(solution)/shard_map/psum | solution.py:77
  591.9 27.4 %scatter_fusion.2 = f32[64,8,128]{2,1,0:T(8,128)} fusion(f32[64,8,128]{2,1,0:T(8,128)} %broadcast.175, s32[256]{0:T(256)S(1)} %bitcast.101, f32[256,128]{1,0:T(8,128)S(1)} %broadcast_multiply_fusion), kind=kCustom, calls=%fused_computation.3 | custom fusion | bytes 395264 | tf_op jit(solution)/shard_map/scatter | solution.py:83
  619.3 5.8 all-to-all-start.2
  657.0 5.3 collective-permute-start.73
  712.6 6.9 collective-permute-done.81
  744.8 6.6 collective-permute-done.87
  775.9 6.6 collective-permute-done.93
  807.7 6.6 collective-permute-done.99
  834.0 5.4 collective-permute-start.104
  839.4 6.6 collective-permute-done.105
  870.9 6.6 collective-permute-done.111
  903.3 6.6 collective-permute-done.117
  933.9 7.1 collective-permute-done.123
  (473 shorter events, 550.6 us)
Async XLA Ops:
  2.0 205.9 %collective-permute-start.6 = (f32[1,48,128]{2,1,0:T(8,128)}, f32[1,48,128]{2,1,0:T(8,128)S(1)}, u32[]{:S(2)}, u32[]{:S(2)}) collective-permute-start(f32[1,48,128]{2,1,0:T(8,128)} %get-tuple-element.136), channel_id=1, source_target_pairs={{16,0},{32,16},{48,32},{64,48},{80,64},{96,80},{112,96},{128,112},... | collective-permute-start | bytes 73736 | tf_op jit(solution)/shard_map/ppermute | solution.py:21
  7.1 170.6 %collective-permute-start.7 = (f32[1,48,128]{2,1,0:T(8,128)S(1)}, f32[1,48,128]{2,1,0:T(8,128)S(1)}, u32[]{:S(2)}, u32[]{:S(2)}) collective-permute-start(f32[1,48,128]{2,1,0:T(8,128)S(1)} %get-tuple-element.137), channel_id=1, source_target_pairs={{0,16},{16,32},{32,48},{48,64},{64,80},{80,96},{96,112},{112,128},... | collective-permute-start | bytes 73736 | tf_op jit(solution)/shard_map/ppermute | solution.py:19
  34.2 125.2 %all-to-all-start = ((s32[64,1,8]{2,1,0:T(1,128)}), s32[64,1,8]{2,1,0:T(1,128)S(1)}, u32[]{:S(2)}, u32[]{:S(2)}) async-start(s32[64,1,8]{2,1,0:T(1,128)} %copy.41), calls=%async_computation | async-start | bytes 65536 | tf_op jit(solution)/shard_map/all_to_all | solution.py:88
  45.2 123.5 %collective-permute-start = (f32[3,1,48,128]{3,2,1,0:T(8,128)S(1)}, f32[3,1,48,128]{3,2,1,0:T(8,128)S(1)}, u32[]{:S(2)}, u32[]{:S(2)}) collective-permute-start(f32[3,1,48,128]{3,2,1,0:T(8,128)S(1)} %get-tuple-element.64), channel_id=1, source_target_pairs={{16,0},{32,16},{48,32},{64,48},{80,64},{96,80},{112,96},{128,112},... | collective-permute-start | bytes 221192 | tf_op jit(solution)/shard_map/ppermute | solution.py:21
  47.5 120.5 %collective-permute-start.1 = (f32[3,1,48,128]{3,2,1,0:T(8,128)S(1)}, f32[3,1,48,128]{3,2,1,0:T(8,128)S(1)}, u32[]{:S(2)}, u32[]{:S(2)}) collective-permute-start(f32[3,1,48,128]{3,2,1,0:T(8,128)S(1)} %get-tuple-element.65), channel_id=1, source_target_pairs={{0,16},{16,32},{32,48},{48,64},{64,80},{80,96},{96,112},{112,128},... | collective-permute-start | bytes 221192 | tf_op jit(solution)/shard_map/ppermute | solution.py:19
  159.4 31.4 %all-to-all-start.1 = ((f32[64,8,128]{2,1,0:T(8,128)}), f32[64,8,128]{2,1,0:T(8,128)}, u32[]{:S(2)}, u32[]{:S(2)}) async-start(f32[64,8,128]{2,1,0:T(8,128)} %scatter_fusion.1), calls=%async_computation.1 | async-start | bytes 524288 | tf_op jit(solution)/shard_map/all_to_all | solution.py:87
  217.1 13.2 %collective-permute-start.14 = (f32[3,18,48,1]{2,3,1,0:T(1,128)S(1)}, f32[3,18,48,1]{2,3,1,0:T(1,128)S(1)}, u32[]{:S(2)}, u32[]{:S(2)}) collective-permute-start(f32[3,18,48,1]{2,3,1,0:T(1,128)S(1)} %copy.43), channel_id=1, source_target_pairs={{4,0},{8,4},{12,8},{5,1},{9,5},{13,9},{6,2},{10,6},{14,10},{7,3},{... | collective-permute-start | bytes 31112 | tf_op jit(solution)/shard_map/ppermute | solution.py:21
  223.5 15.8 %collective-permute-start.9 = (f32[18,48,1]{2,1,0:T(8,128)}, f32[18,48,1]{2,1,0:T(8,128)S(1)}, u32[]{:S(2)}, u32[]{:S(2)}) collective-permute-start(f32[18,48,1]{2,1,0:T(8,128)} %get-tuple-element.102), channel_id=1, source_target_pairs={{4,0},{8,4},{12,8},{5,1},{9,5},{13,9},{6,2},{10,6},{14,10},{7,3},{... | collective-permute-start | bytes 10376 | tf_op jit(solution)/shard_map/ppermute | solution.py:21
  224.7 14.5 %collective-permute-start.8 = (f32[18,48,1]{2,1,0:T(8,128)}, f32[18,48,1]{2,1,0:T(8,128)S(1)}, u32[]{:S(2)}, u32[]{:S(2)}) collective-permute-start(f32[18,48,1]{2,1,0:T(8,128)} %get-tuple-element.103), channel_id=1, source_target_pairs={{0,4},{4,8},{8,12},{1,5},{5,9},{9,13},{2,6},{6,10},{10,14},{3,7},{... | collective-permute-start | bytes 10376 | tf_op jit(solution)/shard_map/ppermute | solution.py:19
  290.4 12.7 %collective-permute-start.27 = (f32[18,48,1]{2,1,0:T(8,128)S(1)}, f32[18,48,1]{2,1,0:T(8,128)S(1)}, u32[]{:S(2)}, u32[]{:S(2)}) collective-permute-start(f32[18,48,1]{2,1,0:T(8,128)S(1)} %get-tuple-element.98), channel_id=1, source_target_pairs={{4,0},{8,4},{12,8},{5,1},{9,5},{13,9},{6,2},{10,6},{14,10},{7,3},{... | collective-permute-start | bytes 10376 | tf_op jit(solution)/shard_map/ppermute | solution.py:21
  291.7 13.1 %collective-permute-start.26 = (f32[18,48,1]{2,1,0:T(8,128)S(1)}, f32[18,48,1]{2,1,0:T(8,128)S(1)}, u32[]{:S(2)}, u32[]{:S(2)}) collective-permute-start(f32[18,48,1]{2,1,0:T(8,128)S(1)} %get-tuple-element.99), channel_id=1, source_target_pairs={{0,4},{4,8},{8,12},{1,5},{5,9},{9,13},{2,6},{6,10},{10,14},{3,7},{... | collective-permute-start | bytes 10376 | tf_op jit(solution)/shard_map/ppermute | solution.py:19
  322.8 12.7 %collective-permute-start.33 = (f32[18,48,1]{2,1,0:T(8,128)S(1)}, f32[18,48,1]{2,1,0:T(8,128)S(1)}, u32[]{:S(2)}, u32[]{:S(2)}) collective-permute-start(f32[18,48,1]{2,1,0:T(8,128)S(1)} %get-tuple-element.96), channel_id=1, source_target_pairs={{4,0},{8,4},{12,8},{5,1},{9,5},{13,9},{6,2},{10,6},{14,10},{7,3},{... | collective-permute-start | bytes 10376 | tf_op jit(solution)/shard_map/ppermute | solution.py:21
  324.1 13.1 %collective-permute-start.32 = (f32[18,48,1]{2,1,0:T(8,128)S(1)}, f32[18,48,1]{2,1,0:T(8,128)S(1)}, u32[]{:S(2)}, u32[]{:S(2)}) collective-permute-start(f32[18,48,1]{2,1,0:T(8,128)S(1)} %get-tuple-element.97), channel_id=1, source_target_pairs={{0,4},{4,8},{8,12},{1,5},{5,9},{9,13},{2,6},{6,10},{10,14},{3,7},{... | collective-permute-start | bytes 10376 | tf_op jit(solution)/shard_map/ppermute | solution.py:19
  356.6 13.1 %collective-permute-start.38 = (f32[18,48,1]{2,1,0:T(8,128)S(1)}, f32[18,48,1]{2,1,0:T(8,128)S(1)}, u32[]{:S(2)}, u32[]{:S(2)}) collective-permute-start(f32[18,48,1]{2,1,0:T(8,128)S(1)} %get-tuple-element.95), channel_id=1, source_target_pairs={{0,4},{4,8},{8,12},{1,5},{5,9},{9,13},{2,6},{6,10},{10,14},{3,7},{... | collective-permute-start | bytes 10376 | tf_op jit(solution)/shard_map/ppermute | solution.py:19
  387.6 13.1 %collective-permute-start.44 = (f32[18,48,1]{2,1,0:T(8,128)S(1)}, f32[18,48,1]{2,1,0:T(8,128)S(1)}, u32[]{:S(2)}, u32[]{:S(2)}) collective-permute-start(f32[18,48,1]{2,1,0:T(8,128)S(1)} %get-tuple-element.93), channel_id=1, source_target_pairs={{0,4},{4,8},{8,12},{1,5},{5,9},{9,13},{2,6},{6,10},{10,14},{3,7},{... | collective-permute-start | bytes 10376 | tf_op jit(solution)/shard_map/ppermute | solution.py:19
  420.2 13.1 %collective-permute-start.50 = (f32[18,48,1]{2,1,0:T(8,128)S(1)}, f32[18,48,1]{2,1,0:T(8,128)S(1)}, u32[]{:S(2)}, u32[]{:S(2)}) collective-permute-start(f32[18,48,1]{2,1,0:T(8,128)S(1)} %get-tuple-element.91), channel_id=1, source_target_pairs={{0,4},{4,8},{8,12},{1,5},{5,9},{9,13},{2,6},{6,10},{10,14},{3,7},{... | collective-permute-start | bytes 10376 | tf_op jit(solution)/shard_map/ppermute | solution.py:19
  452.7 13.1 %collective-permute-start.56 = (f32[18,48,1]{2,1,0:T(8,128)S(1)}, f32[18,48,1]{2,1,0:T(8,128)S(1)}, u32[]{:S(2)}, u32[]{:S(2)}) collective-permute-start(f32[18,48,1]{2,1,0:T(8,128)S(1)} %get-tuple-element.89), channel_id=1, source_target_pairs={{0,4},{4,8},{8,12},{1,5},{5,9},{9,13},{2,6},{6,10},{10,14},{3,7},{... | collective-permute-start | bytes 10376 | tf_op jit(solution)/shard_map/ppermute | solution.py:19
  486.4 12.7 %collective-permute-start.62 = (f32[18,48,1]{2,1,0:T(8,128)S(1)}, f32[18,48,1]{2,1,0:T(8,128)S(1)}, u32[]{:S(2)}, u32[]{:S(2)}) collective-permute-start(f32[18,48,1]{2,1,0:T(8,128)S(1)} %get-tuple-element.87), channel_id=1, source_target_pairs={{4,0},{8,4},{12,8},{5,1},{9,5},{13,9},{6,2},{10,6},{14,10},{7,3},{... | collective-permute-start | bytes 10376 | tf_op jit(solution)/shard_map/ppermute | solution.py:21
  508.7 116.3 %collective-permute-start.67 = (f32[3,1,48,128]{3,2,1,0:T(8,128)S(1)}, f32[3,1,48,128]{3,2,1,0:T(8,128)S(1)}, u32[]{:S(2)}, u32[]{:S(2)}) collective-permute-start(f32[3,1,48,128]{3,2,1,0:T(8,128)S(1)} %get-tuple-element.60), channel_id=1, source_target_pairs={{0,16},{16,32},{32,48},{48,64},{64,80},{80,96},{96,112},{112,128},... | collective-permute-start | bytes 221192 | tf_op jit(solution)/shard_map/ppermute | solution.py:19
  512.4 112.7 %collective-permute-start.66 = (f32[3,1,48,128]{3,2,1,0:T(8,128)S(1)}, f32[3,1,48,128]{3,2,1,0:T(8,128)S(1)}, u32[]{:S(2)}, u32[]{:S(2)}) collective-permute-start(f32[3,1,48,128]{3,2,1,0:T(8,128)S(1)} %get-tuple-element.61), channel_id=1, source_target_pairs={{16,0},{32,16},{48,32},{64,48},{80,64},{96,80},{112,96},{128,112},... | collective-permute-start | bytes 221192 | tf_op jit(solution)/shard_map/ppermute | solution.py:21
  619.3 28.9 %all-to-all-start.2 = ((f32[64,8,128]{2,1,0:T(8,128)}), f32[64,8,128]{2,1,0:T(8,128)}, u32[]{:S(2)}, u32[]{:S(2)}) async-start(f32[64,8,128]{2,1,0:T(8,128)} %scatter_fusion.2), calls=%async_computation.2 | async-start | bytes 524288 | tf_op jit(solution)/shard_map/all_to_all | solution.py:87
  740.0 13.1 %collective-permute-start.86 = (f32[18,48,1]{2,1,0:T(8,128)S(1)}, f32[18,48,1]{2,1,0:T(8,128)S(1)}, u32[]{:S(2)}, u32[]{:S(2)}) collective-permute-start(f32[18,48,1]{2,1,0:T(8,128)S(1)} %get-tuple-element.81), channel_id=1, source_target_pairs={{0,4},{4,8},{8,12},{1,5},{5,9},{9,13},{2,6},{6,10},{10,14},{3,7},{... | collective-permute-start | bytes 10376 | tf_op jit(solution)/shard_map/ppermute | solution.py:19
  769.8 12.8 %collective-permute-start.93 = (f32[18,48,1]{2,1,0:T(8,128)S(1)}, f32[18,48,1]{2,1,0:T(8,128)S(1)}, u32[]{:S(2)}, u32[]{:S(2)}) collective-permute-start(f32[18,48,1]{2,1,0:T(8,128)S(1)} %get-tuple-element.78), channel_id=1, source_target_pairs={{4,0},{8,4},{12,8},{5,1},{9,5},{13,9},{6,2},{10,6},{14,10},{7,3},{... | collective-permute-start | bytes 10376 | tf_op jit(solution)/shard_map/ppermute | solution.py:21
  771.1 13.2 %collective-permute-start.92 = (f32[18,48,1]{2,1,0:T(8,128)S(1)}, f32[18,48,1]{2,1,0:T(8,128)S(1)}, u32[]{:S(2)}, u32[]{:S(2)}) collective-permute-start(f32[18,48,1]{2,1,0:T(8,128)S(1)} %get-tuple-element.79), channel_id=1, source_target_pairs={{0,4},{4,8},{8,12},{1,5},{5,9},{9,13},{2,6},{6,10},{10,14},{3,7},{... | collective-permute-start | bytes 10376 | tf_op jit(solution)/shard_map/ppermute | solution.py:19
  801.3 13.0 %collective-permute-start.99 = (f32[18,48,1]{2,1,0:T(8,128)S(1)}, f32[18,48,1]{2,1,0:T(8,128)S(1)}, u32[]{:S(2)}, u32[]{:S(2)}) collective-permute-start(f32[18,48,1]{2,1,0:T(8,128)S(1)} %get-tuple-element.76), channel_id=1, source_target_pairs={{4,0},{8,4},{12,8},{5,1},{9,5},{13,9},{6,2},{10,6},{14,10},{7,3},{... | collective-permute-start | bytes 10376 | tf_op jit(solution)/shard_map/ppermute | solution.py:21
  802.6 13.5 %collective-permute-start.98 = (f32[18,48,1]{2,1,0:T(8,128)S(1)}, f32[18,48,1]{2,1,0:T(8,128)S(1)}, u32[]{:S(2)}, u32[]{:S(2)}) collective-permute-start(f32[18,48,1]{2,1,0:T(8,128)S(1)} %get-tuple-element.77), channel_id=1, source_target_pairs={{0,4},{4,8},{8,12},{1,5},{5,9},{9,13},{2,6},{6,10},{10,14},{3,7},{... | collective-permute-start | bytes 10376 | tf_op jit(solution)/shard_map/ppermute | solution.py:19
  832.7 13.3 %collective-permute-start.105 = (f32[18,48,1]{2,1,0:T(8,128)S(1)}, f32[18,48,1]{2,1,0:T(8,128)S(1)}, u32[]{:S(2)}, u32[]{:S(2)}) collective-permute-start(f32[18,48,1]{2,1,0:T(8,128)S(1)} %get-tuple-element.74), channel_id=1, source_target_pairs={{4,0},{8,4},{12,8},{5,1},{9,5},{13,9},{6,2},{10,6},{14,10},{7,3},{... | collective-permute-start | bytes 10376 | tf_op jit(solution)/shard_map/ppermute | solution.py:21
  834.0 13.7 %collective-permute-start.104 = (f32[18,48,1]{2,1,0:T(8,128)S(1)}, f32[18,48,1]{2,1,0:T(8,128)S(1)}, u32[]{:S(2)}, u32[]{:S(2)}) collective-permute-start(f32[18,48,1]{2,1,0:T(8,128)S(1)} %get-tuple-element.75), channel_id=1, source_target_pairs={{0,4},{4,8},{8,12},{1,5},{5,9},{9,13},{2,6},{6,10},{10,14},{3,7},{... | collective-permute-start | bytes 10376 | tf_op jit(solution)/shard_map/ppermute | solution.py:19
  866.2 13.1 %collective-permute-start.110 = (f32[18,48,1]{2,1,0:T(8,128)S(1)}, f32[18,48,1]{2,1,0:T(8,128)S(1)}, u32[]{:S(2)}, u32[]{:S(2)}) collective-permute-start(f32[18,48,1]{2,1,0:T(8,128)S(1)} %get-tuple-element.73), channel_id=1, source_target_pairs={{0,4},{4,8},{8,12},{1,5},{5,9},{9,13},{2,6},{6,10},{10,14},{3,7},{... | collective-permute-start | bytes 10376 | tf_op jit(solution)/shard_map/ppermute | solution.py:19
  897.2 12.7 %collective-permute-start.117 = (f32[18,48,1]{2,1,0:T(8,128)S(1)}, f32[18,48,1]{2,1,0:T(8,128)S(1)}, u32[]{:S(2)}, u32[]{:S(2)}) collective-permute-start(f32[18,48,1]{2,1,0:T(8,128)S(1)} %get-tuple-element.70), channel_id=1, source_target_pairs={{4,0},{8,4},{12,8},{5,1},{9,5},{13,9},{6,2},{10,6},{14,10},{7,3},{... | collective-permute-start | bytes 10376 | tf_op jit(solution)/shard_map/ppermute | solution.py:21
  898.5 13.1 %collective-permute-start.116 = (f32[18,48,1]{2,1,0:T(8,128)S(1)}, f32[18,48,1]{2,1,0:T(8,128)S(1)}, u32[]{:S(2)}, u32[]{:S(2)}) collective-permute-start(f32[18,48,1]{2,1,0:T(8,128)S(1)} %get-tuple-element.71), channel_id=1, source_target_pairs={{0,4},{4,8},{8,12},{1,5},{5,9},{9,13},{2,6},{6,10},{10,14},{3,7},{... | collective-permute-start | bytes 10376 | tf_op jit(solution)/shard_map/ppermute | solution.py:19
  932.6 12.7 %collective-permute-start.122 = (f32[18,48,1]{2,1,0:T(8,128)S(1)}, f32[18,48,1]{2,1,0:T(8,128)S(1)}, u32[]{:S(2)}, u32[]{:S(2)}) collective-permute-start(f32[18,48,1]{2,1,0:T(8,128)S(1)} %get-tuple-element.69), channel_id=1, source_target_pairs={{4,0},{8,4},{12,8},{5,1},{9,5},{13,9},{6,2},{10,6},{14,10},{7,3},{... | collective-permute-start | bytes 10376 | tf_op jit(solution)/shard_map/ppermute | solution.py:21
  (139 other events, 1726.6 us)
where the time goes:
time: 975 us; the launch traced here: 958 us
  starting transfers between devices  401 us (41%)
  waiting for transfers between devices  221 us (23%)
  blocking collectives  154 us (16%)
  local copies, waits for them, and re-layouts  123 us (13%)
  other arithmetic  54 us (6%)
    ppermute x63, starting transfers between devices, extended(): lax.ppermute(tail, axis, [(i, (i + 1) % count) for i in range(ends)])  278 us
    ppermute x63, waiting for transfers between devices, extended(): lax.ppermute(head, axis, [((i + 1) % count, i) for i in range(ends)])  168 us
    psum x2, blocking collectives, body(): total = lax.psum(partial_sum, ('gx', 'gy', 'gz'))  154 us
    ppermute x63, starting transfers between devices, extended(): lax.ppermute(head, axis, [((i + 1) % count, i) for i in range(ends)])  98.6 us
    scatter x2, local copies, waits for them, and re-layouts, body(): jnp.zeros((peers, capacity, cells_y), jnp.float32).at[target, slot_index]  54.8 us
    ppermute x63, waiting for transfers between devices, extended(): lax.ppermute(tail, axis, [(i, (i + 1) % count) for i in range(ends)])  53.1 us
    scatter x1, local copies, waits for them, and re-layouts, body(): jnp.zeros((peers, capacity), jnp.int32).at[target, slot_index].set(lines)  21.2 us
  transfers between devices with their start and end apart: 129, of which 70 were waited for; matrix products, arithmetic and copies ran while one was open for 13% of the time, Pallas kernels for 0%

commit v1 on v0

v1 whole, which is shorter than its diff:
```python
import functools

import jax
import jax.numpy as jnp
from jax import lax
from jax.experimental import pallas as pl
from jax.experimental.pallas import tpu as pltpu
from jax.sharding import PartitionSpec as P

BAND = 32
STEPS = 2
SWEEPS = 8
CAP = 8
L = 128
D = 8
MESH = pl.DeviceIdType.MESH
CHUNKS = ((0, 8), (8, 16), (24, 16), (40, 16), (56, 8))
F32 = jnp.float32
BF16 = jnp.bfloat16
DIRS = tuple(
    (dx, dy, dz)
    for dx in (-1, 0, 1)
    for dy in (-1, 0, 1)
    for dz in (-1, 0, 1)
    if (dx, dy, dz) != (0, 0, 0)
)


def lanes(shape):
    return lax.broadcasted_iota(jnp.int32, shape, len(shape) - 1)


def rows_of(shape):
    return lax.broadcasted_iota(jnp.int32, shape, len(shape) - 2)


def pieces(x):
    hi = x.astype(BF16)
    rest = x - hi.astype(F32)
    mid = rest.astype(BF16)
    return hi, mid, (rest - mid.astype(F32)).astype(BF16)


def kernel(
    sizes,
    vel,
    prs,
    kern,
    own_r,
    line_r,
    turb_r,
    cnt,
    thrust,
    infx,
    infy,
    vout,
    pout,
    W,
    wys,
    wyr,
    wzs,
    wzr,
    E,
    ST,
    sys_,
    syr,
    szs,
    szr,
    E2,
    R,
    GS,
    gys,
    gyr,
    BGS,
    F,
    fys,
    fyr,
    BF,
    S,
    PR,
    S1,
    R1,
    S2,
    R2,
    LC,
    TC,
    O,
    KC,
    TB,
    u1s,
    u1r,
    u2s,
    u2r,
    in_sem,
    face_send,
    face_recv,
    star_send,
    star_recv,
    gs_send,
    gs_recv,
    f_send,
    f_recv,
    row_send,
    row_recv,
    u_send,
    u_recv,
):
    NGX, NGY, NGZ, CX, CZ = sizes
    Z = CZ + 2 * D
    X = CX + 2 * D
    NG = CX // 8
    T = thrust.shape[1]
    rows = kern.shape[0]
    peers = NGX * NGY
    slots = peers * CAP
    plane = NGY * NGZ
    gx = lax.axis_index("gx")
    gy = lax.axis_index("gy")
    gz = lax.axis_index("gz")
    own_z = pl.ds(D, CZ)

    def near(dx, dy, dz):
        return (
            lax.rem(gx + dx + NGX, NGX),
            lax.rem(gy + dy + NGY, NGY),
            lax.rem(gz + dz + NGZ, NGZ),
        )

    def plane_peer(r):
        spot = lax.rem(gy * NGZ + gz + r, plane)
        return (gx, spot // NGZ, lax.rem(spot, NGZ))

    def line_peer(r):
        return (lax.rem(gx + r, NGX), gy, gz)

    def remote(src, dst, send, recv, device):
        return pltpu.make_async_remote_copy(
            src_ref=src,
            dst_ref=dst,
            send_sem=send,
            recv_sem=recv,
            device_id=device,
            device_id_type=MESH,
        )

    loads = [
        pltpu.make_async_copy(vel, W.at[pl.ds(0, 3), pl.ds(1, CX), own_z, :], in_sem.at[0]),
        pltpu.make_async_copy(prs, W.at[3, pl.ds(1, CX), own_z, :], in_sem.at[1]),
    ]
    for load in loads:
        load.start()
    barrier = pltpu.get_barrier_semaphore()

    @pl.loop(1, plane)
    def _(r):
        pl.semaphore_signal(barrier, inc=1, device_id=plane_peer(r), device_id_type=MESH)

    @pl.loop(1, NGX)
    def _(r):
        pl.semaphore_signal(barrier, inc=1, device_id=line_peer(r), device_id_type=MESH)

    greeted = plane - 1 + NGX - 1
    for d in DIRS:
        if d[0] and (d[1] or d[2]):
            pl.semaphore_signal(barrier, inc=1, device_id=near(*d), device_id_type=MESH)
            greeted += 1

    owner = own_r[...]
    live = lanes((1, rows)) < cnt[...]
    spot = jnp.where(live, (owner % NGY) * NGX + owner // NGY, -1)
    land = (rows_of((peers, rows)) == spot).astype(F32)
    before = (rows_of((rows, rows)) < lanes((rows, rows))).astype(BF16)
    earlier = jnp.dot(land.astype(BF16), before, preferred_element_type=F32)
    rank = jnp.sum(land * earlier, axis=0, keepdims=True).astype(jnp.int32)
    slot = jnp.where(live, spot * CAP + rank, -1)
    place = (rows_of((slots, rows)) == slot).astype(BF16)
    hi, mid, lo = pieces(kern[...])
    both = jnp.dot(place, jnp.concatenate([hi, mid], axis=1), preferred_element_type=F32)
    sorted_rows = both[:, :L] + both[:, L:]
    sorted_rows = sorted_rows + jnp.dot(place, lo, preferred_element_type=F32)
    kind = rows_of((L, rows))
    line = line_r[...]
    told = jnp.where(kind < 8, line // 32, jnp.where(kind < 16, line % 32, turb_r[...]))
    told = jnp.where((kind % 8 == rank) & (kind < 24), told, 0).astype(F32).astype(BF16)
    meta = lax.dot_general(
        land.astype(BF16), told, (((1,), (1,)), ((), ())), preferred_element_type=F32
    )
    for k in range(NGY):
        S1[k, : NGX * CAP, :] = sorted_rows[k * NGX * CAP : (k + 1) * NGX * CAP]
        S1[k, NGX * CAP :, :] = meta[k * NGX : (k + 1) * NGX]
    TB[...] = jnp.zeros_like(TB)
    TB[0, 0:1, :T] = infx[...].astype(F32)
    TB[1, 0:1, :T] = infy[...].astype(F32)
    TB[2, 0:1, :T] = thrust[...]
    zero_pad = jnp.zeros((8, L), F32)
    for pp in range(2):
        for ab in range(2):

            @pl.loop(0, X)
            def _(x):
                PR[pp, ab, x, 0:8, :] = zero_pad
                PR[pp, ab, x, Z + 8 : Z + 16, :] = zero_pad

    BF[0, :, :] = jnp.zeros((Z, L), F32)
    BF[X + 1, :, :] = jnp.zeros((Z, L), F32)
    for load in loads:
        load.wait()
    pl.semaphore_wait(barrier, greeted)

    def row_first(r):
        peer = lax.rem(gy + r, NGY)
        return remote(
            S1.at[peer], R1.at[r - 1], row_send.at[r - 1], row_recv.at[r - 1], (gx, peer, gz)
        )

    for r in range(1, NGY):
        row_first(r).start()
    R1[NGY - 1] = S1[gy]

    lane = lanes((CZ, L))

    def face_copies(step):
        nc = 4 if step == 0 else 3
        comps = pl.ds(0, nc)
        many = pl.ds(0, nc * CX)
        return [
            remote(
                W.at[comps, pl.ds(CX, 1), own_z, :],
                W.at[comps, pl.ds(0, 1), own_z, :],
                face_send.at[0],
                face_recv.at[0],
                near(1, 0, 0),
            ),
            remote(
                W.at[comps, pl.ds(1, 1), own_z, :],
                W.at[comps, pl.ds(CX + 1, 1), own_z, :],
                face_send.at[1],
                face_recv.at[1],
                near(-1, 0, 0),
            ),
            remote(wys, wyr.at[0], face_send.at[2], face_recv.at[2], near(0, 1, 0)),
            remote(wys, wyr.at[1], face_send.at[3], face_recv.at[3], near(0, -1, 0)),
            remote(
                wzs.at[1, many], wzr.at[0, many], face_send.at[4], face_recv.at[4], near(0, 0, 1)
            ),
            remote(
                wzs.at[0, many], wzr.at[1, many], face_send.at[5], face_recv.at[5], near(0, 0, -1)
            ),
        ]

    def edge_lanes(q):
        return (lane == 2 * q) | (lane == lax.rem(2 * q + L - 1, L))

    def send_faces(step):
        nc = 4 if step == 0 else 3
        copies = face_copies(step)
        copies[0].start()
        copies[1].start()
        for c in range(nc):
            wzs[0, c * CX : (c + 1) * CX, :] = W[c, 1 : CX + 1, D, :]
            wzs[1, c * CX : (c + 1) * CX, :] = W[c, 1 : CX + 1, D + CZ - 1, :]
        copies[4].start()
        copies[5].start()
        packed = jnp.zeros((CZ, L), F32)
        for c in range(nc):

            def pack(x, kept, c=c):
                q = c * CX + x
                turned = pltpu.roll(W[c, 1 + x, own_z, :], 2 * q, 1)
                return jnp.where(edge_lanes(q), turned, kept)

            packed = lax.fori_loop(0, CX, pack, packed)
        wys[...] = packed
        copies[2].start()
        copies[3].start()
        return copies

    def merged(received):
        right = jnp.where(gy < NGY - 1, received[1], 0.0)
        left = jnp.where(gy > 0, received[0], 0.0)
        return jnp.where(lane % 2 == 0, right, pltpu.roll(left, 2, 1))

    def wait_faces(step, copies):
        nc = 4 if step == 0 else 3
        for copy in copies:
            copy.wait()
        E[...] = merged(wyr)
        for c in range(nc):
            W[c, 0, own_z, :] = jnp.where(gx > 0, W[c, 0, own_z, :], 0.0)
            W[c, CX + 1, own_z, :] = jnp.where(gx < NGX - 1, W[c, CX + 1, own_z, :], 0.0)
            above = jnp.where(gz > 0, wzr[0, c * CX : (c + 1) * CX, :], 0.0)
            below = jnp.where(gz < NGZ - 1, wzr[1, c * CX : (c + 1) * CX, :], 0.0)
            W[c, 1 : CX + 1, D - 1, :] = above
            W[c, 1 : CX + 1, D + CZ, :] = below

    def sides(cells, edge):
        left = jnp.where(lane == 0, edge, pltpu.roll(cells, 1, 1))
        right = jnp.where(lane == L - 1, edge, pltpu.roll(cells, L - 1, 1))
        return left, right

    def edge_of(ref, q):
        return pltpu.roll(ref[...], lax.rem(2 * L - 1 - 2 * q, L), 1)

    def star_faces(step):
        nc = 4 if step == 0 else 3
        for c in range(nc):

            @pl.loop(0, CX)
            def _(x):
                cells = W[c, 1 + x, own_z, :]
                left, right = sides(cells, edge_of(E, c * CX + x))
                total = W[c, x, own_z, :] + W[c, x + 2, own_z, :]
                total = total + W[c, 1 + x, pl.ds(D - 1, CZ), :] + W[c, 1 + x, pl.ds(D + 1, CZ), :]
                total = total + left + right
                if c < 3:
                    ST[c, 1 + x, own_z, :] = 0.88 * cells + 0.02 * total
                else:
                    R[x] = total

        copies = [
            remote(
                ST.at[0, CX, own_z, :],
                ST.at[0, 0, own_z, :],
                star_send.at[0],
                star_recv.at[0],
                near(1, 0, 0),
            ),
            remote(
                ST.at[0, 1, own_z, :],
                ST.at[0, CX + 1, own_z, :],
                star_send.at[1],
                star_recv.at[1],
                near(-1, 0, 0),
            ),
            remote(sys_, syr.at[0], star_send.at[2], star_recv.at[2], near(0, 1, 0)),
            remote(sys_, syr.at[1], star_send.at[3], star_recv.at[3], near(0, -1, 0)),
            remote(szs.at[1], szr.at[0], star_send.at[4], star_recv.at[4], near(0, 0, 1)),
            remote(szs.at[0], szr.at[1], star_send.at[5], star_recv.at[5], near(0, 0, -1)),
        ]
        copies[0].start()
        copies[1].start()
        szs[0] = ST[2, 1 : CX + 1, D, :]
        szs[1] = ST[2, 1 : CX + 1, D + CZ - 1, :]
        copies[4].start()
        copies[5].start()

        def pack(x, kept):
            turned = pltpu.roll(ST[1, 1 + x, own_z, :], 2 * x, 1)
            return jnp.where(edge_lanes(x), turned, kept)

        sys_[...] = lax.fori_loop(0, CX, pack, jnp.zeros((CZ, L), F32))
        copies[2].start()
        copies[3].start()
        return copies

    def around(j):
        return lax.rem(lane - 16 * j + 8 + L, L) < 16

    def sources(step, copies):
        for copy in copies:
            copy.wait()
        E2[...] = merged(syr)
        ST[0, 0, own_z, :] = jnp.where(gx > 0, ST[0, 0, own_z, :], 0.0)
        ST[0, CX + 1, own_z, :] = jnp.where(gx < NGX - 1, ST[0, CX + 1, own_z, :], 0.0)
        ST[2, 1 : CX + 1, D - 1, :] = jnp.where(gz > 0, szr[0], 0.0)
        ST[2, 1 : CX + 1, D + CZ, :] = jnp.where(gz < NGZ - 1, szr[1], 0.0)
        for group in range(NG):

            def one(j, kept, group=group):
                x = group * 8 + j
                left, right = sides(ST[1, 1 + x, own_z, :], edge_of(E2, x))
                total = ST[0, x + 2, own_z, :] - ST[0, x, own_z, :] + right - left
                total = total + ST[2, 1 + x, pl.ds(D + 1, CZ), :]
                source = 0.5 * (total - ST[2, 1 + x, pl.ds(D - 1, CZ), :])
                first = R[x] - source
                GS[step, 0, D + x, own_z, :] = first
                GS[step, 1, D + x, own_z, :] = source
                mine = around(j)
                return (
                    jnp.where(mine, pltpu.roll(first, 16 * j, 1), kept[0]),
                    jnp.where(mine, pltpu.roll(source, 16 * j, 1), kept[1]),
                )

            nothing = jnp.zeros((CZ, L), F32)
            kept = lax.fori_loop(0, 8, one, (nothing, nothing))
            gys[0, group] = kept[0]
            gys[1, group] = kept[1]

    def deep_copies(cells, off, packed, received, send, recv):
        fields = pl.ds(0, packed.shape[0])
        copies = []
        for i, (dx, dy, dz) in enumerate(DIRS):
            if dy == 0:
                zs, zd = {
                    0: (own_z, own_z),
                    -1: (pl.ds(D, D), pl.ds(D + CZ, D)),
                    1: (pl.ds(CZ, D), pl.ds(0, D)),
                }[dz]
                deep = off if dz == 0 else D
                xs, xd = {
                    0: (pl.ds(off, CX), pl.ds(off, CX)),
                    -1: (pl.ds(off, deep), pl.ds(off + CX, deep)),
                    1: (pl.ds(off + CX - deep, deep), pl.ds(off - deep, deep)),
                }[dx]
                src = cells.at[fields, xs, zs, :]
                dst = cells.at[fields, xd, zd, :]
            else:
                zs, zd = {
                    0: (pl.ds(0, CZ), own_z),
                    -1: (pl.ds(0, D), pl.ds(D + CZ, D)),
                    1: (pl.ds(CZ - D, D), pl.ds(0, D)),
                }[dz]
                xs, xd = {
                    0: (pl.ds(0, NG), pl.ds(1, NG)),
                    -1: (pl.ds(0, 1), pl.ds(NG + 1, 1)),
                    1: (pl.ds(NG - 1, 1), pl.ds(0, 1)),
                }[dx]
                src = packed.at[fields, xs, zs, :]
                dst = received.at[0 if dy == 1 else 1, fields, xd, zd, :]
            copies.append(remote(src, dst, send.at[i], recv.at[i], near(dx, dy, dz)))
        return copies

    lane_z = lanes((Z, L))

    def unpacked(received, field, x):
        group, j = x // 8, lax.rem(x, 8)
        both_sides = jnp.where(
            lane_z % 16 < 8, received[1, field, group], received[0, field, group]
        )
        return pltpu.roll(both_sides, lax.rem(L - 16 * j, L), 1)

    def one_wait(whole_src, whole_dst, send, recv, device):
        remote(whole_src, whole_dst, send, recv, device).wait()

    def inflow_first(step):
        column = jnp.sum(W[0, 1 : CX + 1, own_z, :], axis=1)
        y = rows_of((L, L)) + gy * L
        begin = TB[1, 0:1, :].astype(jnp.int32)
        band = ((y >= begin) & (y < begin + BAND)).astype(F32)
        sums = jnp.dot(column, band, precision=lax.Precision.HIGHEST, preferred_element_type=F32)
        x = rows_of((CX, L)) + gx * CX
        picked = jnp.where(x == TB[0, 0:1, :].astype(jnp.int32), sums, 0.0)
        u1s[step] = jnp.broadcast_to(jnp.sum(picked, axis=0, keepdims=True), (8, L))

        @pl.loop(1, plane)
        def _(r):
            remote(
                u1s.at[step],
                u1r.at[step, r - 1],
                u_send.at[2 * step],
                u_recv.at[2 * step],
                plane_peer(r),
            ).start()

    def inflow_second(step):
        whole = u1r.at[step]
        one_wait(whole, whole, u_send.at[2 * step], u_recv.at[2 * step], plane_peer(1))
        u2s[step] = u1s[step] + jnp.sum(u1r[step], axis=0)

        @pl.loop(1, NGX)
        def _(r):
            remote(
                u2s.at[step],
                u2r.at[step, r - 1],
                u_send.at[2 * step + 1],
                u_recv.at[2 * step + 1],
                line_peer(r),
            ).start()

    def magnitudes(step):
        whole = u2r.at[step]
        one_wait(whole, whole, u_send.at[2 * step + 1], u_recv.at[2 * step + 1], line_peer(1))
        total = u2s[step] + jnp.sum(u2r[step], axis=0)
        uref = total[0:1] * (1.0 / (BAND * CZ * NGZ))
        return 0.5 * TB[2, 0:1, :] * uref * jnp.abs(uref)

    def forces(step):
        size = magnitudes(step)

        @pl.loop(0, NGX)
        def _(g):
            at = pl.ds(pl.multiple_of(g * CAP * NGY, CAP * NGY), CAP * NGY)
            hot = jnp.where(TC[at, :] == lanes((CAP * NGY, L)).astype(F32), size, 0.0)
            scaled = R2[g, : CAP * NGY, :] * jnp.sum(hot, axis=1, keepdims=True)
            top = scaled.astype(BF16)
            KC[at, :L] = top
            KC[at, L:] = (scaled - top.astype(F32)).astype(BF16)

        part = CX // 4
        for h in range(4):
            both = jnp.dot(
                O[h * part * CZ : (h + 1) * part * CZ, :], KC[...], preferred_element_type=F32
            )
            force = (both[:, :L] + both[:, L:]).reshape(part, CZ, L)
            F[0, D + 1 + h * part : D + 1 + (h + 1) * part, own_z, :] = force
        for group in range(NG):

            def pack(j, kept, group=group):
                turned = pltpu.roll(F[0, D + 1 + group * 8 + j, own_z, :], 16 * j, 1)
                return jnp.where(around(j), turned, kept)

            fys[0, group] = lax.fori_loop(0, 8, pack, jnp.zeros((CZ, L), F32))
        copies = deep_copies(F, D + 1, fys, fyr, f_send, f_recv)
        for copy in copies:
            copy.start()
        return copies

    def inside(x):
        spot_x = gx * CX + x - D
        return (spot_x >= 0) & (spot_x < NGX * CX)

    ringlane = lanes((8, L))[0:1]
    right_ok = jnp.where(gy < NGY - 1, 1.0, 0.0)
    left_ok = jnp.where(gy > 0, 1.0, 0.0)
    ring = jnp.where(ringlane < D, right_ok, jnp.where(ringlane >= L - D, left_ok, 0.0))
    top_ok = jnp.where(gz > 0, 1.0, 0.0)
    bottom_ok = jnp.where(gz < NGZ - 1, 1.0, 0.0)

    def weights(x):
        base = jnp.where(inside(x), 1.0 / 6.0, 0.0)
        out = []
        for start, size in CHUNKS:
            scale = base
            if start == 0:
                scale = base * top_ok
            if start + size == Z:
                scale = base * bottom_ok
            out.append((scale, ring * scale))
        return out

    def ring_sides(a, b):
        lane_c = lanes(a.shape)
        am, bm = pltpu.roll(a, 1, 1), pltpu.roll(b, 1, 1)
        ap, bp = pltpu.roll(a, L - 1, 1), pltpu.roll(b, L - 1, 1)
        first, last = lane_c == 0, lane_c == L - 1
        return (
            (jnp.where(first, bm, am), jnp.where(last, bp, ap)),
            (jnp.where(first, am, bm), jnp.where(last, ap, bp)),
        )

    def sweeps(step, f_copies):
        for copy in f_copies:
            copy.wait()

        @pl.loop(0, X)
        def _(x):
            BF[x + 1] = unpacked(fyr, 0, x)

        @pl.loop(0, X)
        def _(x):
            plus = jnp.where(inside(x + 1), -0.2, 0.0)
            minus = jnp.where(inside(x - 1), -0.2, 0.0)
            scales = weights(x)
            for (start, size), (ca, cb) in zip(CHUNKS, scales):
                at = pl.ds(start, size)
                to = pl.ds(start + 8, size)
                fa = plus * F[0, x + 2, at, :] - minus * F[0, x, at, :]
                fb = plus * BF[x + 2, at, :] - minus * BF[x, at, :]
                S[0, x, at, :] = GS[step, 1, x, at, :] + fa
                S[1, x, at, :] = BGS[1, x, at, :] + fb
                PR[0, 0, x, to, :] = (GS[step, 0, x, at, :] - fa) * ca
                PR[0, 1, x, to, :] = (BGS[0, x, at, :] - fb) * cb

        for k in range(2, SWEEPS + 1):
            src, dst = k % 2, (k + 1) % 2
            deep = SWEEPS + 1 - k

            @pl.loop(D - deep, D + CX + deep)
            def _(x):
                scales = weights(x)
                for (start, size), (ca, cb) in zip(CHUNKS, scales):
                    at = pl.ds(start + 8, size)
                    up = pl.ds(start + 7, size)
                    down = pl.ds(start + 9, size)
                    a_sides, b_sides = ring_sides(PR[src, 0, x, at, :], PR[src, 1, x, at, :])
                    for ab, (left, right), scale in ((0, a_sides, ca), (1, b_sides, cb)):
                        total = PR[src, ab, x - 1, at, :] + PR[src, ab, x + 1, at, :]
                        total = total + PR[src, ab, x, up, :] + PR[src, ab, x, down, :]
                        total = total + (left + right)
                        total = total - S[ab, x, pl.ds(start, size), :]
                        PR[dst, ab, x, at, :] = total * scale

        at = pl.ds(D + 8, CZ)
        last = (SWEEPS + 1) % 2

        @pl.loop(0, CX)
        def _(x):
            deep = D + x
            (left, right), _ = ring_sides(PR[last, 0, deep, at, :], PR[last, 1, deep, at, :])
            back, ahead = PR[last, 0, deep - 1, at, :], PR[last, 0, deep + 1, at, :]
            up = PR[last, 0, deep, pl.ds(D + 7, CZ), :]
            down = PR[last, 0, deep, pl.ds(D + 9, CZ), :]
            force = F[0, D + 1 + x, own_z, :]
            W[0, 1 + x, own_z, :] = ST[0, 1 + x, own_z, :] - 0.4 * force - 0.5 * (ahead - back)
            W[1, 1 + x, own_z, :] = ST[1, 1 + x, own_z, :] - 0.5 * (right - left)
            W[2, 1 + x, own_z, :] = ST[2, 1 + x, own_z, :] - 0.5 * (down - up)
            if step == 0:
                R[x] = back + ahead + up + down + left + right

    def unpack_sources(step, copies):
        for copy in copies:
            copy.wait()
        for field in range(2):

            @pl.loop(0, X)
            def _(x):
                BGS[field, x] = unpacked(gyr.at[step], field, x)

    def row_second():
        for r in range(1, NGY):
            row_first(r).wait()

        @pl.loop(0, NGX)
        def _(d):
            for k in range(NGY):
                at = pl.ds(pl.multiple_of(d * CAP, CAP), CAP)
                S2[d, k * CAP : (k + 1) * CAP, :] = R1[k, at, :]
                S2[d, NGY * CAP + k : NGY * CAP + k + 1, :] = R1[k, pl.ds(NGX * CAP + d, 1), :]

        @pl.loop(1, NGX)
        def _(r):
            peer = lax.rem(gx + r, NGX)
            remote(
                S2.at[peer], R2.at[r - 1], row_send.at[NGY], row_recv.at[NGY], (peer, gy, gz)
            ).start()

        R2[NGX - 1] = S2[gx]

    def row_last():
        whole = R2.at[pl.ds(0, NGX - 1)]
        one_wait(whole, whole, row_send.at[NGY], row_recv.at[NGY], line_peer(1))
        which = lanes((CAP, L)) - rows_of((CAP, L))

        @pl.loop(0, NGX)
        def _(g):
            for k in range(NGY):
                row = R2[g, NGY * CAP + k : NGY * CAP + k + 1, :]
                told_line = jnp.where(which == 0, 32.0 * row, jnp.where(which == 8, row, 0.0))
                told_turbine = jnp.where(which == 16, row, 0.0)
                at = pl.ds(pl.multiple_of((g * NGY + k) * CAP, CAP), CAP)
                LC[at, :] = jnp.broadcast_to(
                    jnp.sum(told_line, axis=1, keepdims=True), (CAP, L)
                )
                TC[at, :] = jnp.broadcast_to(
                    jnp.sum(told_turbine, axis=1, keepdims=True), (CAP, L)
                )

        wide = min(L, slots)
        same = rows_of((wide, wide)) == lanes((wide, wide))
        for c in range(slots // wide):
            turned = jnp.where(same, LC[c * wide : (c + 1) * wide, :wide], 0.0)
            named = jnp.sum(turned, axis=0, keepdims=True).astype(jnp.int32)

            @pl.loop(0, CX)
            def _(x):
                at = pl.ds(pl.multiple_of(x * CZ, CZ), CZ)
                hit = rows_of((CZ, wide)) + x * CZ == named
                O[at, c * wide : (c + 1) * wide] = hit.astype(F32).astype(BF16)

    for step in range(STEPS):
        faces = send_faces(step)
        inflow_first(step)
        wait_faces(step, faces)
        stars = star_faces(step)
        if step == 0:
            row_second()
        inflow_second(step)
        sources(step, stars)
        deep = deep_copies(GS.at[step], D, gys, gyr.at[step], gs_send.at[step], gs_recv.at[step])
        for copy in deep:
            copy.start()
        if step == 0:
            row_last()
        f_copies = forces(step)
        unpack_sources(step, deep)
        sweeps(step, f_copies)

    last = (SWEEPS + 1) % 2
    outs = [
        pltpu.make_async_copy(W.at[pl.ds(0, 3), pl.ds(1, CX), own_z, :], vout, in_sem.at[0]),
        pltpu.make_async_copy(
            PR.at[last, 0, pl.ds(D, CX), pl.ds(D + 8, CZ), :], pout, in_sem.at[1]
        ),
    ]
    for out in outs:
        out.start()
    for out in outs:
        out.wait()


def body(
    shape,
    velocity,
    pressure,
    kern,
    owners,
    lines,
    point_turbine,
    row_counts,
    thrust,
    inflow_x,
    inflow_y,
):
    ngx, ngy, ngz = shape
    cx, cz = velocity.shape[1:3]
    z, x, ng = cz + 2 * D, cx + 2 * D, cx // 8
    rows = kern.shape[0]
    slots = ngx * ngy * CAP
    turbines = thrust.shape[0]
    any_spec = pl.BlockSpec(memory_space=pl.ANY)
    vmem_spec = pl.BlockSpec(memory_space=pltpu.VMEM)
    vm = pltpu.VMEM
    dma = pltpu.SemaphoreType.DMA
    meta = max(8, ngy)
    scratch = [
        vm((4, cx + 2, z, L), F32),
        vm((cz, L), F32),
        vm((2, cz, L), F32),
        vm((2, 4 * cx, L), F32),
        vm((2, 4 * cx, L), F32),
        vm((cz, L), F32),
        vm((3, cx + 2, z, L), F32),
        vm((cz, L), F32),
        vm((2, cz, L), F32),
        vm((2, cx, L), F32),
        vm((2, cx, L), F32),
        vm((cz, L), F32),
        vm((cx, cz, L), F32),
        vm((STEPS, 2, x, z, L), F32),
        vm((2, ng, cz, L), F32),
        vm((STEPS, 2, 2, ng + 2, z, L), F32),
        vm((2, x, z, L), F32),
        vm((1, x + 2, z, L), F32),
        vm((1, ng, cz, L), F32),
        vm((2, 1, ng + 2, z, L), F32),
        vm((x + 2, z, L), F32),
        vm((2, x, z, L), F32),
        vm((2, 2, x, z + 16, L), F32),
        vm((ngy, ngx * CAP + ngx, L), F32),
        vm((ngy, ngx * CAP + ngx, L), F32),
        vm((ngx, ngy * CAP + meta, L), F32),
        vm((ngx, ngy * CAP + meta, L), F32),
        vm((slots, L), F32),
        vm((slots, L), F32),
        vm((cx * cz, slots), BF16),
        vm((slots, 2 * L), BF16),
        vm((3, 8, L), F32),
        vm((STEPS, 8, L), F32),
        vm((STEPS, ngy * ngz - 1, 8, L), F32),
        vm((STEPS, 8, L), F32),
        vm((STEPS, ngx - 1, 8, L), F32),
        dma((2,)),
        dma((6,)),
        dma((6,)),
        dma((6,)),
        dma((6,)),
        dma((STEPS, 26)),
        dma((STEPS, 26)),
        dma((26,)),
        dma((26,)),
        dma((ngy + 1,)),
        dma((ngy + 1,)),
        dma((2 * STEPS,)),
        dma((2 * STEPS,)),
    ]
    return pl.pallas_call(
        functools.partial(kernel, (ngx, ngy, ngz, cx, cz)),
        out_shape=(
            jax.ShapeDtypeStruct(velocity.shape, F32),
            jax.ShapeDtypeStruct(pressure.shape, F32),
        ),
        in_specs=[any_spec] * 2 + [vmem_spec] * 8,
        out_specs=(any_spec, any_spec),
        scratch_shapes=scratch,
        compiler_params=pltpu.CompilerParams(
            collective_id=0, has_side_effects=True, vmem_limit_bytes=56 * 1024 * 1024
        ),
    )(
        velocity,
        pressure,
        kern,
        owners.reshape(1, rows),
        lines.reshape(1, rows),
        point_turbine.reshape(1, rows),
        row_counts.reshape(1, 1),
        thrust.reshape(1, turbines),
        inflow_x.reshape(1, turbines),
        inflow_y.reshape(1, turbines),
    )


def solution(mesh):
    placed = (
        P(None, "gx", "gz", "gy"),
        P("gx", "gz", "gy"),
        P(("gx", "gy", "gz"), None),
        P(("gx", "gy", "gz"), None),
        P(("gx", "gy", "gz")),
        P(("gx", "gy", "gz")),
        P("gx", "gy", "gz"),
        P(),
        P(),
        P(),
    )
    shape = (mesh.shape["gx"], mesh.shape["gy"], mesh.shape["gz"])
    return jax.shard_map(
        functools.partial(body, shape),
        mesh=mesh,
        in_specs=placed,
        out_specs=(P(None, "gx", "gz", "gy"), P("gx", "gz", "gy")),
        check_vma=False,
    )
```

time: 975 us -> 140 us (0.14); the launches traced: 958 us -> 140 us
  starting transfers between devices: 401 us -> 0 us
  waiting for transfers between devices: 221 us -> 0 us
  blocking collectives: 154 us -> 0 us
  Pallas kernels: 0 us -> 135 us
  local copies, waits for them, and re-layouts: 123 us -> 3.16 us
  other arithmetic: 54 us -> 0 us
    ppermute x126 -> x0, starting transfers between devices: 377 us -> none  [the longest x63 278 us: extended(): lax.ppermute(tail, axis, [(i, (i + 1) % count) for i in range(ends)])]
    ppermute x126 -> x0, waiting for transfers between devices: 221 us -> none  [the longest x63 168 us: extended(): lax.ppermute(head, axis, [((i + 1) % count, i) for i in range(ends)])]
    psum x2 -> x0, blocking collectives: 154 us -> none  [body(): total = lax.psum(partial_sum, ('gx', 'gy', 'gz'))]
    pallas_call x0 -> x1, Pallas kernels: none -> 135 us  [body(): pl.pallas_call(functools.partial(kernel, (ngx, ngy, ngz, cx, cz)), out_sh...]
    scatter x3 -> x0, local copies, waits for them, and re-layouts: 76 us -> none  [the longest x2 54.8 us: body(): jnp.zeros((peers, capacity, cells_y), jnp.float32).at[target, slot_index]]
    slice x54 -> x0, local copies, waits for them, and re-layouts: 27.4 us -> none  [the longest x23 17 us: extended(): head = lax.slice_in_dim(cells, 0, width, axis=dim)]
    all_to_all x3 -> x0, starting transfers between devices: 23.9 us -> none  [the longest x2 13 us: body(): lax.all_to_all(send_values, ('gx', 'gy'), split_axis=0, concat_axis=0, ti...]
    div x16 -> x0, other arithmetic: 13.7 us -> none  [body(): press = (neighbours(pressure_faces(press)) - source) / 6.0]
  transfers between devices with their start and end apart: 129 -> 0, of which waited for: 70 -> 0; matrix products, arithmetic and copies ran while one was open for 13% -> 0% of each run, Pallas kernels for 0% -> 0%
where the time goes in v1:
time: 140 us
  Pallas kernels  135 us (96%)
  local copies, waits for them, and re-layouts  3.16 us (2%)
    pallas_call x1, Pallas kernels, body(): pl.pallas_call(functools.partial(kernel, (ngx, ngy, ngz, cx, cz)), out_sh...  135 us
    unnamed x4, local copies, waits for them, and re-layouts  3.16 us

profile of v1, /device:TPU:1, one launch (start us, length us, event | category | flops | bytes accessed | tf_op | source)
XLA Modules:
  0.0 139.6 jit_solution(4980687681054807199)
XLA Ops:
  1.3 135.2 %shard_map.113 = (f32[3,16,48,128]{3,2,1,0:T(8,128)}, f32[16,48,128]{2,1,0:T(8,128)}) custom-call(f32[3,16,48,128]{3,2,1,0:T(8,128)} %vel.1, f32[16,48,128]{2,1,0:T(8,128)} %prs.1, f32[256,128]{1,0:T(8,128)} %kern.1, s32[1,256]{1,0:T(1,128)} %bitcast.8, s32[1,256]{1,0:T(1,128)} %bitcast.9, s32[1,256]{1,0:T(1,128)} %bitcast.10, s32[1,1]{1,0:T(1,128)} %bitcast.7.cnt, ...), custom_call_target="tpu_custom_call" | custom-call | tf_op jit(solution)/shard_map/pallas_call | solution.py:766
  136.5 0.0 copy-start
  136.5 2.4 %copy.15 = f32[3,16,48,128]{3,2,1,0:T(8,128)} copy(f32[3,16,48,128]{3,2,1,0:T(8,128)} %get-tuple-element.4) | data formatting | bytes 2359296
  138.9 0.0 copy-done
  138.9 0.7 copy.16
Async XLA Ops:
  136.5 2.4 %copy-start = (f32[16,48,128]{2,1,0:T(8,128)S(1)}, f32[16,48,128]{2,1,0:T(8,128)}, u32[]{:S(2)}) copy-start(f32[16,48,128]{2,1,0:T(8,128)} %get-tuple-element.5) | copy-start | bytes 1179652

commit v2 on v1

--- a/solution.py
+++ b/solution.py
@@ -13,6 +13,7 @@
 CAP = 8
 L = 128
 D = 8
+BLOCK = 4
 MESH = pl.DeviceIdType.MESH
 CHUNKS = ((0, 8), (8, 16), (24, 16), (40, 16), (56, 8))
 F32 = jnp.float32
@@ -196,10 +197,13 @@
     for pp in range(2):
         for ab in range(2):
 
-            @pl.loop(0, X)
+            @pl.loop(0, X + 2, unroll=X + 2)
             def _(x):
                 PR[pp, ab, x, 0:8, :] = zero_pad
                 PR[pp, ab, x, Z + 8 : Z + 16, :] = zero_pad
+
+            PR[pp, ab, 0, :, :] = jnp.zeros((Z + 16, L), F32)
+            PR[pp, ab, X + 1, :, :] = jnp.zeros((Z + 16, L), F32)
 
     BF[0, :, :] = jnp.zeros((Z, L), F32)
     BF[X + 1, :, :] = jnp.zeros((Z, L), F32)
@@ -248,8 +252,11 @@
             ),
         ]
 
+    def turn(cells, by):
+        return pltpu.roll(cells, by % L, 1) if by % L else cells
+
     def edge_lanes(q):
-        return (lane == 2 * q) | (lane == lax.rem(2 * q + L - 1, L))
+        return (lane == 2 * q) | (lane == (2 * q + L - 1) % L)
 
     def send_faces(step):
         nc = 4 if step == 0 else 3
@@ -264,12 +271,10 @@
         packed = jnp.zeros((CZ, L), F32)
         for c in range(nc):
 
-            def pack(x, kept, c=c):
+            for x in range(CX):
                 q = c * CX + x
-                turned = pltpu.roll(W[c, 1 + x, own_z, :], 2 * q, 1)
-                return jnp.where(edge_lanes(q), turned, kept)
-
-            packed = lax.fori_loop(0, CX, pack, packed)
+                turned = pltpu.roll(W[c, 1 + x, own_z, :], 2 * q, 1) if q else W[c, 1, own_z, :]
+                packed = jnp.where(edge_lanes(q), turned, packed)
         wys[...] = packed
         copies[2].start()
         copies[3].start()
@@ -299,13 +304,13 @@
         return left, right
 
     def edge_of(ref, q):
-        return pltpu.roll(ref[...], lax.rem(2 * L - 1 - 2 * q, L), 1)
+        return pltpu.roll(ref[...], (2 * L - 1 - 2 * q) % L, 1)
 
     def star_faces(step):
         nc = 4 if step == 0 else 3
         for c in range(nc):
 
-            @pl.loop(0, CX)
+            @pl.loop(0, CX, unroll=8)
             def _(x):
                 cells = W[c, 1 + x, own_z, :]
                 left, right = sides(cells, edge_of(E, c * CX + x))
@@ -344,17 +349,17 @@
         copies[4].start()
         copies[5].start()
 
-        def pack(x, kept):
-            turned = pltpu.roll(ST[1, 1 + x, own_z, :], 2 * x, 1)
-            return jnp.where(edge_lanes(x), turned, kept)
-
-        sys_[...] = lax.fori_loop(0, CX, pack, jnp.zeros((CZ, L), F32))
+        packed = jnp.zeros((CZ, L), F32)
+        for x in range(CX):
+            turned = pltpu.roll(ST[1, 1 + x, own_z, :], 2 * x, 1) if x else ST[1, 1, own_z, :]
+            packed = jnp.where(edge_lanes(x), turned, packed)
+        sys_[...] = packed
         copies[2].start()
         copies[3].start()
         return copies
 
     def around(j):
-        return lax.rem(lane - 16 * j + 8 + L, L) < 16
+        return (lane + (8 - 16 * j) % L) % L < 16
 
     def sources(step, copies):
         for copy in copies:
@@ -366,7 +371,8 @@
         ST[2, 1 : CX + 1, D + CZ, :] = jnp.where(gz < NGZ - 1, szr[1], 0.0)
         for group in range(NG):
 
-            def one(j, kept, group=group):
+            kept = [jnp.zeros((CZ, L), F32), jnp.zeros((CZ, L), F32)]
+            for j in range(8):
                 x = group * 8 + j
                 left, right = sides(ST[1, 1 + x, own_z, :], edge_of(E2, x))
                 total = ST[0, x + 2, own_z, :] - ST[0, x, own_z, :] + right - left
@@ -376,13 +382,8 @@
                 GS[step, 0, D + x, own_z, :] = first
                 GS[step, 1, D + x, own_z, :] = source
                 mine = around(j)
-                return (
-                    jnp.where(mine, pltpu.roll(first, 16 * j, 1), kept[0]),
-                    jnp.where(mine, pltpu.roll(source, 16 * j, 1), kept[1]),
-                )
-
-            nothing = jnp.zeros((CZ, L), F32)
-            kept = lax.fori_loop(0, 8, one, (nothing, nothing))
+                kept[0] = jnp.where(mine, turn(first, 16 * j), kept[0])
+                kept[1] = jnp.where(mine, turn(source, 16 * j), kept[1])
             gys[0, group] = kept[0]
             gys[1, group] = kept[1]
 
@@ -422,12 +423,14 @@
 
     lane_z = lanes((Z, L))
 
-    def unpacked(received, field, x):
-        group, j = x // 8, lax.rem(x, 8)
-        both_sides = jnp.where(
-            lane_z % 16 < 8, received[1, field, group], received[0, field, group]
-        )
-        return pltpu.roll(both_sides, lax.rem(L - 16 * j, L), 1)
+    def unpack(received, field, target, base):
+        @pl.loop(0, NG + 2)
+        def _(group):
+            both_sides = jnp.where(
+                lane_z % 16 < 8, received[1, field, group], received[0, field, group]
+            )
+            for j in range(8):
+                target[base + group * 8 + j] = turn(both_sides, -16 * j)
 
     def one_wait(whole_src, whole_dst, send, recv, device):
         remote(whole_src, whole_dst, send, recv, device).wait()
@@ -477,7 +480,7 @@
     def forces(step):
         size = magnitudes(step)
 
-        @pl.loop(0, NGX)
+        @pl.loop(0, NGX, unroll=4)
         def _(g):
             at = pl.ds(pl.multiple_of(g * CAP * NGY, CAP * NGY), CAP * NGY)
             hot = jnp.where(TC[at, :] == lanes((CAP * NGY, L)).astype(F32), size, 0.0)
@@ -495,11 +498,11 @@
             F[0, D + 1 + h * part : D + 1 + (h + 1) * part, own_z, :] = force
         for group in range(NG):
 
-            def pack(j, kept, group=group):
-                turned = pltpu.roll(F[0, D + 1 + group * 8 + j, own_z, :], 16 * j, 1)
-                return jnp.where(around(j), turned, kept)
-
-            fys[0, group] = lax.fori_loop(0, 8, pack, jnp.zeros((CZ, L), F32))
+            kept = jnp.zeros((CZ, L), F32)
+            for j in range(8):
+                turned = turn(F[0, D + 1 + group * 8 + j, own_z, :], 16 * j)
+                kept = jnp.where(around(j), turned, kept)
+            fys[0, group] = kept
         copies = deep_copies(F, D + 1, fys, fyr, f_send, f_recv)
         for copy in copies:
             copy.start()
@@ -516,22 +519,29 @@
     top_ok = jnp.where(gz > 0, 1.0, 0.0)
     bottom_ok = jnp.where(gz < NGZ - 1, 1.0, 0.0)
 
-    def weights(x):
-        base = jnp.where(inside(x), 1.0 / 6.0, 0.0)
+    def weights():
         out = []
         for start, size in CHUNKS:
-            scale = base
+            scale = 1.0 / 6.0
             if start == 0:
-                scale = base * top_ok
+                scale = scale * top_ok
             if start + size == Z:
-                scale = base * bottom_ok
+                scale = scale * bottom_ok
             out.append((scale, ring * scale))
         return out
 
+    def outside_x(pp):
+        for ok, x in ((gx > 0, D), (gx < NGX - 1, D + CX + 1)):
+
+            @pl.when(jnp.logical_not(ok))
+            def _():
+                for ab in range(2):
+                    PR[pp, ab, x, 8 : 8 + Z, :] = jnp.zeros((Z, L), F32)
+
     def ring_sides(a, b):
-        lane_c = lanes(a.shape)
-        am, bm = pltpu.roll(a, 1, 1), pltpu.roll(b, 1, 1)
-        ap, bp = pltpu.roll(a, L - 1, 1), pltpu.roll(b, L - 1, 1)
+        axis, lane_c = a.ndim - 1, lanes(a.shape)
+        am, bm = pltpu.roll(a, 1, axis), pltpu.roll(b, 1, axis)
+        ap, bp = pltpu.roll(a, L - 1, axis), pltpu.roll(b, L - 1, axis)
         first, last = lane_c == 0, lane_c == L - 1
         return (
             (jnp.where(first, bm, am), jnp.where(last, bp, ap)),
@@ -542,15 +552,13 @@
         for copy in f_copies:
             copy.wait()
 
-        @pl.loop(0, X)
-        def _(x):
-            BF[x + 1] = unpacked(fyr, 0, x)
-
-        @pl.loop(0, X)
+        unpack(fyr, 0, BF, 1)
+        scales = weights()
+
+        @pl.loop(0, X, unroll=4)
         def _(x):
             plus = jnp.where(inside(x + 1), -0.2, 0.0)
             minus = jnp.where(inside(x - 1), -0.2, 0.0)
-            scales = weights(x)
             for (start, size), (ca, cb) in zip(CHUNKS, scales):
                 at = pl.ds(start, size)
                 to = pl.ds(start + 8, size)
@@ -558,34 +566,38 @@
                 fb = plus * BF[x + 2, at, :] - minus * BF[x, at, :]
                 S[0, x, at, :] = GS[step, 1, x, at, :] + fa
                 S[1, x, at, :] = BGS[1, x, at, :] + fb
-                PR[0, 0, x, to, :] = (GS[step, 0, x, at, :] - fa) * ca
-                PR[0, 1, x, to, :] = (BGS[0, x, at, :] - fb) * cb
-
+                PR[0, 0, x + 1, to, :] = (GS[step, 0, x, at, :] - fa) * ca
+                PR[0, 1, x + 1, to, :] = (BGS[0, x, at, :] - fb) * cb
+
+        outside_x(0)
         for k in range(2, SWEEPS + 1):
             src, dst = k % 2, (k + 1) % 2
-            deep = SWEEPS + 1 - k
-
-            @pl.loop(D - deep, D + CX + deep)
-            def _(x):
-                scales = weights(x)
+            wide = -(-(CX + 2 * (SWEEPS + 1 - k)) // BLOCK) * BLOCK
+            begin = (X - wide) // 2
+
+            @pl.loop(0, wide // BLOCK)
+            def _(block):
+                x = begin + block * BLOCK
+                mid, back, ahead = pl.ds(x + 1, BLOCK), pl.ds(x, BLOCK), pl.ds(x + 2, BLOCK)
                 for (start, size), (ca, cb) in zip(CHUNKS, scales):
                     at = pl.ds(start + 8, size)
                     up = pl.ds(start + 7, size)
                     down = pl.ds(start + 9, size)
-                    a_sides, b_sides = ring_sides(PR[src, 0, x, at, :], PR[src, 1, x, at, :])
+                    a_sides, b_sides = ring_sides(PR[src, 0, mid, at, :], PR[src, 1, mid, at, :])
                     for ab, (left, right), scale in ((0, a_sides, ca), (1, b_sides, cb)):
-                        total = PR[src, ab, x - 1, at, :] + PR[src, ab, x + 1, at, :]
-                        total = total + PR[src, ab, x, up, :] + PR[src, ab, x, down, :]
-                        total = total + (left + right)
-                        total = total - S[ab, x, pl.ds(start, size), :]
-                        PR[dst, ab, x, at, :] = total * scale
+                        total = PR[src, ab, back, at, :] + PR[src, ab, ahead, at, :]
+                        total = total + PR[src, ab, mid, up, :] + PR[src, ab, mid, down, :]
+                        total = total - S[ab, pl.ds(x, BLOCK), pl.ds(start, size), :]
+                        PR[dst, ab, mid, at, :] = (total + (left + right)) * scale
+
+            outside_x(dst)
 
         at = pl.ds(D + 8, CZ)
         last = (SWEEPS + 1) % 2
 
-        @pl.loop(0, CX)
+        @pl.loop(0, CX, unroll=4)
         def _(x):
-            deep = D + x
+            deep = D + x + 1
             (left, right), _ = ring_sides(PR[last, 0, deep, at, :], PR[last, 1, deep, at, :])
             back, ahead = PR[last, 0, deep - 1, at, :], PR[last, 0, deep + 1, at, :]
             up = PR[last, 0, deep, pl.ds(D + 7, CZ), :]
@@ -601,10 +613,7 @@
         for copy in copies:
             copy.wait()
         for field in range(2):
-
-            @pl.loop(0, X)
-            def _(x):
-                BGS[field, x] = unpacked(gyr.at[step], field, x)
+            unpack(gyr.at[step], field, BGS.at[field], 0)
 
     def row_second():
         for r in range(1, NGY):
@@ -631,7 +640,7 @@
         one_wait(whole, whole, row_send.at[NGY], row_recv.at[NGY], line_peer(1))
         which = lanes((CAP, L)) - rows_of((CAP, L))
 
-        @pl.loop(0, NGX)
+        @pl.loop(0, NGX, unroll=4)
         def _(g):
             for k in range(NGY):
                 row = R2[g, NGY * CAP + k : NGY * CAP + k + 1, :]
@@ -679,7 +688,7 @@
     outs = [
         pltpu.make_async_copy(W.at[pl.ds(0, 3), pl.ds(1, CX), own_z, :], vout, in_sem.at[0]),
         pltpu.make_async_copy(
-            PR.at[last, 0, pl.ds(D, CX), pl.ds(D + 8, CZ), :], pout, in_sem.at[1]
+            PR.at[last, 0, pl.ds(D + 1, CX), pl.ds(D + 8, CZ), :], pout, in_sem.at[1]
         ),
     ]
     for out in outs:
@@ -735,7 +744,7 @@
         vm((2, 1, ng + 2, z, L), F32),
         vm((x + 2, z, L), F32),
         vm((2, x, z, L), F32),
-        vm((2, 2, x, z + 16, L), F32),
+        vm((2, 2, x + 2, z + 16, L), F32),
         vm((ngy, ngx * CAP + ngx, L), F32),
         vm((ngy, ngx * CAP + ngx, L), F32),
         vm((ngx, ngy * CAP + meta, L), F32),

time: 140 us -> 97.6 us (0.70)
  Pallas kernels: 135 us -> 92.9 us
    pallas_call x1, Pallas kernels: 135 us -> 92.9 us  [body(): pl.pallas_call(functools.partial(kernel, (ngx, ngy, ngz, cx, cz)), out_sh...]
where the time goes in v2:
time: 97.6 us; the launch traced here: 97.4 us
  Pallas kernels  92.9 us (95%)
  local copies, waits for them, and re-layouts  3.16 us (3%)
  between operations  1.3 us (1%)
    pallas_call x1, Pallas kernels, body(): pl.pallas_call(functools.partial(kernel, (ngx, ngy, ngz, cx, cz)), out_sh...  92.9 us
    unnamed x4, local copies, waits for them, and re-layouts  3.16 us

profile of v2, /device:TPU:1, one launch (start us, length us, event | category | flops | bytes accessed | tf_op | source)
XLA Modules:
  0.0 97.4 jit_solution(12567330775114006068)
XLA Ops:
  1.3 92.9 %shard_map.113 = (f32[3,16,48,128]{3,2,1,0:T(8,128)}, f32[16,48,128]{2,1,0:T(8,128)}) custom-call(f32[3,16,48,128]{3,2,1,0:T(8,128)} %vel.1, f32[16,48,128]{2,1,0:T(8,128)} %prs.1, f32[256,128]{1,0:T(8,128)} %kern.1, s32[1,256]{1,0:T(1,128)} %bitcast.8, s32[1,256]{1,0:T(1,128)} %bitcast.9, s32[1,256]{1,0:T(1,128)} %bitcast.10, s32[1,1]{1,0:T(1,128)} %bitcast.7.cnt, ...), custom_call_target="tpu_custom_call" | custom-call | tf_op jit(solution)/shard_map/pallas_call | solution.py:775
  94.2 0.0 copy-start
  94.2 2.4 %copy.15 = f32[3,16,48,128]{3,2,1,0:T(8,128)} copy(f32[3,16,48,128]{3,2,1,0:T(8,128)} %get-tuple-element.4) | data formatting | bytes 2359296
  96.6 0.0 copy-done
  96.7 0.7 copy.16
Async XLA Ops:
  94.2 2.4 %copy-start = (f32[16,48,128]{2,1,0:T(8,128)S(1)}, f32[16,48,128]{2,1,0:T(8,128)}, u32[]{:S(2)}) copy-start(f32[16,48,128]{2,1,0:T(8,128)} %get-tuple-element.5) | copy-start | bytes 1179652

commit v3 on v2

--- a/solution.py
+++ b/solution.py
@@ -19,11 +19,16 @@
 F32 = jnp.float32
 BF16 = jnp.bfloat16
 DIRS = tuple(
-    (dx, dy, dz)
-    for dx in (-1, 0, 1)
-    for dy in (-1, 0, 1)
-    for dz in (-1, 0, 1)
-    if (dx, dy, dz) != (0, 0, 0)
+    sorted(
+        (
+            (dx, dy, dz)
+            for dx in (-1, 0, 1)
+            for dy in (-1, 0, 1)
+            for dz in (-1, 0, 1)
+            if (dx, dy, dz) != (0, 0, 0)
+        ),
+        key=lambda d: (abs(d[1]), abs(d[2]), -abs(d[0])),
+    )
 )
 
 
@@ -46,6 +51,16 @@
     sizes,
     vel,
     prs,
+    kern_h,
+    own_h,
+    line_h,
+    turb_h,
+    cnt_h,
+    thrust_h,
+    infx_h,
+    infy_h,
+    vout,
+    pout,
     kern,
     own_r,
     line_r,
@@ -54,8 +69,6 @@
     thrust,
     infx,
     infy,
-    vout,
-    pout,
     W,
     wys,
     wyr,
@@ -88,6 +101,7 @@
     O,
     KC,
     TB,
+    RING,
     u1s,
     u1r,
     u2s,
@@ -148,7 +162,22 @@
         pltpu.make_async_copy(vel, W.at[pl.ds(0, 3), pl.ds(1, CX), own_z, :], in_sem.at[0]),
         pltpu.make_async_copy(prs, W.at[3, pl.ds(1, CX), own_z, :], in_sem.at[1]),
     ]
-    for load in loads:
+    small = [
+        pltpu.make_async_copy(source, here, in_sem.at[2 + i])
+        for i, (source, here) in enumerate(
+            (
+                (own_h, own_r),
+                (line_h, line_r),
+                (turb_h, turb_r),
+                (cnt_h, cnt),
+                (kern_h, kern),
+                (thrust_h, thrust),
+                (infx_h, infx),
+                (infy_h, infy),
+            )
+        )
+    ]
+    for load in small + loads:
         load.start()
     barrier = pltpu.get_barrier_semaphore()
 
@@ -166,6 +195,8 @@
             pl.semaphore_signal(barrier, inc=1, device_id=near(*d), device_id_type=MESH)
             greeted += 1
 
+    for load in small:
+        load.wait()
     owner = own_r[...]
     live = lanes((1, rows)) < cnt[...]
     spot = jnp.where(live, (owner % NGY) * NGX + owner // NGY, -1)
@@ -193,20 +224,6 @@
     TB[0, 0:1, :T] = infx[...].astype(F32)
     TB[1, 0:1, :T] = infy[...].astype(F32)
     TB[2, 0:1, :T] = thrust[...]
-    zero_pad = jnp.zeros((8, L), F32)
-    for pp in range(2):
-        for ab in range(2):
-
-            @pl.loop(0, X + 2, unroll=X + 2)
-            def _(x):
-                PR[pp, ab, x, 0:8, :] = zero_pad
-                PR[pp, ab, x, Z + 8 : Z + 16, :] = zero_pad
-
-            PR[pp, ab, 0, :, :] = jnp.zeros((Z + 16, L), F32)
-            PR[pp, ab, X + 1, :, :] = jnp.zeros((Z + 16, L), F32)
-
-    BF[0, :, :] = jnp.zeros((Z, L), F32)
-    BF[X + 1, :, :] = jnp.zeros((Z, L), F32)
     for load in loads:
         load.wait()
     pl.semaphore_wait(barrier, greeted)
@@ -538,6 +555,14 @@
                 for ab in range(2):
                     PR[pp, ab, x, 8 : 8 + Z, :] = jnp.zeros((Z, L), F32)
 
+    def beside(a, b):
+        both = jnp.concatenate([a, b], axis=-1).reshape(-1, 2 * L)
+        top = both.astype(BF16)
+        rest = (both - top.astype(F32)).astype(BF16)
+        total = jnp.dot(top, RING[...], preferred_element_type=F32)
+        total = total + jnp.dot(rest, RING[...], preferred_element_type=F32)
+        return total[:, :L].reshape(a.shape), total[:, L:].reshape(a.shape)
+
     def ring_sides(a, b):
         axis, lane_c = a.ndim - 1, lanes(a.shape)
         am, bm = pltpu.roll(a, 1, axis), pltpu.roll(b, 1, axis)
@@ -575,20 +600,21 @@
             wide = -(-(CX + 2 * (SWEEPS + 1 - k)) // BLOCK) * BLOCK
             begin = (X - wide) // 2
 
-            @pl.loop(0, wide // BLOCK)
+            @pl.loop(0, wide // BLOCK, unroll=True)
             def _(block):
                 x = begin + block * BLOCK
                 mid, back, ahead = pl.ds(x + 1, BLOCK), pl.ds(x, BLOCK), pl.ds(x + 2, BLOCK)
+                along = beside(PR[src, 0, mid, 8 : 8 + Z, :], PR[src, 1, mid, 8 : 8 + Z, :])
                 for (start, size), (ca, cb) in zip(CHUNKS, scales):
                     at = pl.ds(start + 8, size)
                     up = pl.ds(start + 7, size)
                     down = pl.ds(start + 9, size)
-                    a_sides, b_sides = ring_sides(PR[src, 0, mid, at, :], PR[src, 1, mid, at, :])
-                    for ab, (left, right), scale in ((0, a_sides, ca), (1, b_sides, cb)):
+                    for ab, scale in ((0, ca), (1, cb)):
                         total = PR[src, ab, back, at, :] + PR[src, ab, ahead, at, :]
                         total = total + PR[src, ab, mid, up, :] + PR[src, ab, mid, down, :]
                         total = total - S[ab, pl.ds(x, BLOCK), pl.ds(start, size), :]
-                        PR[dst, ab, mid, at, :] = (total + (left + right)) * scale
+                        total = total + along[ab][:, start : start + size]
+                        PR[dst, ab, mid, at, :] = total * scale
 
             outside_x(dst)
 
@@ -666,9 +692,29 @@
                 hit = rows_of((CZ, wide)) + x * CZ == named
                 O[at, c * wide : (c + 1) * wide] = hit.astype(F32).astype(BF16)
 
+    def constants():
+        zero_pad = jnp.zeros((8, L), F32)
+        for pp in range(2):
+            for ab in range(2):
+
+                @pl.loop(0, X + 2, unroll=X + 2)
+                def _(x):
+                    PR[pp, ab, x, 0:8, :] = zero_pad
+                    PR[pp, ab, x, Z + 8 : Z + 16, :] = zero_pad
+
+                PR[pp, ab, 0, :, :] = jnp.zeros((Z + 16, L), F32)
+                PR[pp, ab, X + 1, :, :] = jnp.zeros((Z + 16, L), F32)
+
+        BF[0, :, :] = jnp.zeros((Z, L), F32)
+        BF[X + 1, :, :] = jnp.zeros((Z, L), F32)
+        step_apart = lax.rem(rows_of((2 * L, 2 * L)) - lanes((2 * L, 2 * L)) + 2 * L, 2 * L)
+        RING[...] = ((step_apart == 1) | (step_apart == 2 * L - 1)).astype(F32).astype(BF16)
+
     for step in range(STEPS):
         faces = send_faces(step)
         inflow_first(step)
+        if step == 0:
+            constants()
         wait_faces(step, faces)
         stars = star_faces(step)
         if step == 0:
@@ -695,6 +741,25 @@
         out.start()
     for out in outs:
         out.wait()
+
+
+def deliver(vel, prs, vout, pout, held, load_sem, store_sem):
+    half = prs.shape[0] // 2
+    loads, stores = [], []
+    for k in range(8):
+        at = pl.ds(k % 2 * half, half)
+        source, target = (vel.at[k // 2, at], vout.at[k // 2, at])
+        if k >= 6:
+            source, target = prs.at[at], pout.at[at]
+        loads.append(pltpu.make_async_copy(source, held.at[k], load_sem.at[k]))
+        stores.append(pltpu.make_async_copy(held.at[k], target, store_sem.at[k]))
+    for load in loads:
+        load.start()
+    for load, store in zip(loads, stores):
+        load.wait()
+        store.start()
+    for store in stores:
+        store.wait()
 
 
 def body(
@@ -717,11 +782,19 @@
     slots = ngx * ngy * CAP
     turbines = thrust.shape[0]
     any_spec = pl.BlockSpec(memory_space=pl.ANY)
-    vmem_spec = pl.BlockSpec(memory_space=pltpu.VMEM)
     vm = pltpu.VMEM
     dma = pltpu.SemaphoreType.DMA
     meta = max(8, ngy)
+    i32 = jnp.int32
     scratch = [
+        vm((rows, L), F32),
+        vm((1, rows), i32),
+        vm((1, rows), i32),
+        vm((1, rows), i32),
+        vm((1, 1), i32),
+        vm((1, turbines), F32),
+        vm((1, turbines), i32),
+        vm((1, turbines), i32),
         vm((4, cx + 2, z, L), F32),
         vm((cz, L), F32),
         vm((2, cz, L), F32),
@@ -754,11 +827,12 @@
         vm((cx * cz, slots), BF16),
         vm((slots, 2 * L), BF16),
         vm((3, 8, L), F32),
+        vm((2 * L, 2 * L), BF16),
         vm((STEPS, 8, L), F32),
         vm((STEPS, ngy * ngz - 1, 8, L), F32),
         vm((STEPS, 8, L), F32),
         vm((STEPS, ngx - 1, 8, L), F32),
-        dma((2,)),
+        dma((10,)),
         dma((6,)),
         dma((6,)),
         dma((6,)),
@@ -772,13 +846,13 @@
         dma((2 * STEPS,)),
         dma((2 * STEPS,)),
     ]
-    return pl.pallas_call(
+    ahead = pl.pallas_call(
         functools.partial(kernel, (ngx, ngy, ngz, cx, cz)),
         out_shape=(
             jax.ShapeDtypeStruct(velocity.shape, F32),
             jax.ShapeDtypeStruct(pressure.shape, F32),
         ),
-        in_specs=[any_spec] * 2 + [vmem_spec] * 8,
+        in_specs=[pl.BlockSpec(memory_space=pltpu.HBM)] * 10,
         out_specs=(any_spec, any_spec),
         scratch_shapes=scratch,
         compiler_params=pltpu.CompilerParams(
@@ -796,6 +870,17 @@
         inflow_x.reshape(1, turbines),
         inflow_y.reshape(1, turbines),
     )
+    return pl.pallas_call(
+        deliver,
+        out_shape=(
+            jax.ShapeDtypeStruct(velocity.shape, F32),
+            jax.ShapeDtypeStruct(pressure.shape, F32),
+        ),
+        in_specs=[any_spec] * 2,
+        out_specs=(any_spec, any_spec),
+        scratch_shapes=[vm((8, cx // 2, cz, L), F32), dma((8,)), dma((8,))],
+        compiler_params=pltpu.CompilerParams(vmem_limit_bytes=60 * 1024 * 1024),
+    )(*ahead)
 
 
 def solution(mesh):

time: 97.6 us -> 88.3 us (0.905)
  Pallas kernels: 92.9 us -> 86.7 us
  local copies, waits for them, and re-layouts: 3.16 us -> 0 us
    pallas_call x1, Pallas kernels: 92.9 us -> 84.4 us  [body(): pl.pallas_call(functools.partial(kernel, (ngx, ngy, ngz, cx, cz)), out_sh...]
    unnamed x4 -> x0, local copies, waits for them, and re-layouts: 3.16 us -> none
    pallas_call x0 -> x1, Pallas kernels: none -> 2.29 us  [body(): pl.pallas_call(deliver, out_shape=(jax.ShapeDtypeStruct(velocity.shape, F...]
where the time goes in v3:
time: 88.3 us; the launch traced here: 88.2 us
  Pallas kernels  86.7 us (98%)
  between operations  1.45 us (2%)
    pallas_call x1, Pallas kernels, body(): pl.pallas_call(functools.partial(kernel, (ngx, ngy, ngz, cx, cz)), out_sh...  84.4 us
    pallas_call x1, Pallas kernels, body(): pl.pallas_call(deliver, out_shape=(jax.ShapeDtypeStruct(velocity.shape, F...  2.29 us

profile of v3, /device:TPU:1, one launch (start us, length us, event | category | flops | bytes accessed | tf_op | source)
XLA Modules:
  0.0 88.2 jit_solution(1738738605656304272)
XLA Ops:
  1.3 84.4 %shard_map.113 = (f32[3,16,48,128]{3,2,1,0:T(8,128)}, f32[16,48,128]{2,1,0:T(8,128)}) custom-call(f32[3,16,48,128]{3,2,1,0:T(8,128)} %vel.1, f32[16,48,128]{2,1,0:T(8,128)} %prs.1, f32[256,128]{1,0:T(8,128)} %kern_h.1, s32[1,256]{1,0:T(1,128)} %bitcast.8, s32[1,256]{1,0:T(1,128)} %bitcast.9, s32[1,256]{1,0:T(1,128)} %bitcast.10, s32[1,1]{1,0:T(1,128)} %bitcast.7.cnt_h, ...), custom_call_target="tpu_custom_call" | custom-call | tf_op jit(solution)/shard_map/pallas_call | solution.py:849
  85.7 2.3 %shard_map.114 = (f32[3,16,48,128]{3,2,1,0:T(8,128)}, f32[16,48,128]{2,1,0:T(8,128)}) custom-call(f32[3,16,48,128]{3,2,1,0:T(8,128)} %get-tuple-element.4.vel, f32[16,48,128]{2,1,0:T(8,128)} %get-tuple-element.5.prs), custom_call_target="tpu_custom_call" | custom-call | tf_op jit(solution)/shard_map/pallas_call | solution.py:873

commit v4 on v3

--- a/solution.py
+++ b/solution.py
@@ -217,9 +217,12 @@
     meta = lax.dot_general(
         land.astype(BF16), told, (((1,), (1,)), ((), ())), preferred_element_type=F32
     )
+    hx = NGX // 2
     for k in range(NGY):
-        S1[k, : NGX * CAP, :] = sorted_rows[k * NGX * CAP : (k + 1) * NGX * CAP]
-        S1[k, NGX * CAP :, :] = meta[k * NGX : (k + 1) * NGX]
+        for h in range(2):
+            first = k * NGX + h * hx
+            S1[k, h, : hx * CAP, :] = sorted_rows[first * CAP : (first + hx) * CAP]
+            S1[k, h, hx * CAP :, :] = meta[first : first + hx]
     TB[...] = jnp.zeros_like(TB)
     TB[0, 0:1, :T] = infx[...].astype(F32)
     TB[1, 0:1, :T] = infy[...].astype(F32)
@@ -228,14 +231,16 @@
         load.wait()
     pl.semaphore_wait(barrier, greeted)
 
-    def row_first(r):
+    def row_first(r, h):
         peer = lax.rem(gy + r, NGY)
+        i = 2 * (r - 1) + h
         return remote(
-            S1.at[peer], R1.at[r - 1], row_send.at[r - 1], row_recv.at[r - 1], (gx, peer, gz)
+            S1.at[peer, h], R1.at[r - 1, h], row_send.at[i], row_recv.at[i], (gx, peer, gz)
         )
 
-    for r in range(1, NGY):
-        row_first(r).start()
+    for h in range(2):
+        for r in range(1, NGY):
+            row_first(r, h).start()
     R1[NGY - 1] = S1[gy]
 
     lane = lanes((CZ, L))
@@ -641,37 +646,52 @@
         for field in range(2):
             unpack(gyr.at[step], field, BGS.at[field], 0)
 
-    def row_second():
+    row_all = 2 * (NGY - 1)
+
+    def row_second(h):
         for r in range(1, NGY):
-            row_first(r).wait()
-
-        @pl.loop(0, NGX)
+            row_first(r, h).wait()
+
+        @pl.loop(0, hx)
         def _(d):
+            notes = R1[0, h, pl.ds(hx * CAP + d, 1), :]
             for k in range(NGY):
                 at = pl.ds(pl.multiple_of(d * CAP, CAP), CAP)
-                S2[d, k * CAP : (k + 1) * CAP, :] = R1[k, at, :]
-                S2[d, NGY * CAP + k : NGY * CAP + k + 1, :] = R1[k, pl.ds(NGX * CAP + d, 1), :]
-
-        @pl.loop(1, NGX)
-        def _(r):
-            peer = lax.rem(gx + r, NGX)
-            remote(
-                S2.at[peer], R2.at[r - 1], row_send.at[NGY], row_recv.at[NGY], (peer, gy, gz)
-            ).start()
-
-        R2[NGX - 1] = S2[gx]
+                S2[h * hx + d, k * CAP : (k + 1) * CAP, :] = R1[k, h, at, :]
+                if k:
+                    more = R1[k, h, pl.ds(hx * CAP + d, 1), :]
+                    notes = jnp.where(lanes((1, L)) // 32 == k, pltpu.roll(more, 32 * k, 1), notes)
+            S2[h * hx + d, NGY * CAP : NGY * CAP + 1, :] = notes
+
+        @pl.loop(h * hx, (h + 1) * hx)
+        def _(peer):
+            @pl.when(peer != gx)
+            def _():
+                slot = lax.rem(peer - gx + NGX, NGX) - 1
+                remote(
+                    S2.at[peer],
+                    R2.at[slot],
+                    row_send.at[row_all],
+                    row_recv.at[row_all],
+                    (peer, gy, gz),
+                ).start()
+
+        if h == 1:
+            R2[NGX - 1] = S2[gx]
 
     def row_last():
         whole = R2.at[pl.ds(0, NGX - 1)]
-        one_wait(whole, whole, row_send.at[NGY], row_recv.at[NGY], line_peer(1))
+        one_wait(whole, whole, row_send.at[row_all], row_recv.at[row_all], line_peer(1))
         which = lanes((CAP, L)) - rows_of((CAP, L))
 
         @pl.loop(0, NGX, unroll=4)
         def _(g):
             for k in range(NGY):
-                row = R2[g, NGY * CAP + k : NGY * CAP + k + 1, :]
-                told_line = jnp.where(which == 0, 32.0 * row, jnp.where(which == 8, row, 0.0))
-                told_turbine = jnp.where(which == 16, row, 0.0)
+                row = R2[g, NGY * CAP : NGY * CAP + 1, :]
+                base = 32 * k
+                coarse = jnp.where(which == base, 32.0 * row, 0.0)
+                told_line = jnp.where(which == base + 8, row, coarse)
+                told_turbine = jnp.where(which == base + 16, row, 0.0)
                 at = pl.ds(pl.multiple_of((g * NGY + k) * CAP, CAP), CAP)
                 LC[at, :] = jnp.broadcast_to(
                     jnp.sum(told_line, axis=1, keepdims=True), (CAP, L)
@@ -715,10 +735,11 @@
         inflow_first(step)
         if step == 0:
             constants()
+            row_second(0)
         wait_faces(step, faces)
+        if step == 0:
+            row_second(1)
         stars = star_faces(step)
-        if step == 0:
-            row_second()
         inflow_second(step)
         sources(step, stars)
         deep = deep_copies(GS.at[step], D, gys, gyr.at[step], gs_send.at[step], gs_recv.at[step])
@@ -784,7 +805,6 @@
     any_spec = pl.BlockSpec(memory_space=pl.ANY)
     vm = pltpu.VMEM
     dma = pltpu.SemaphoreType.DMA
-    meta = max(8, ngy)
     i32 = jnp.int32
     scratch = [
         vm((rows, L), F32),
@@ -818,10 +838,10 @@
         vm((x + 2, z, L), F32),
         vm((2, x, z, L), F32),
         vm((2, 2, x + 2, z + 16, L), F32),
-        vm((ngy, ngx * CAP + ngx, L), F32),
-        vm((ngy, ngx * CAP + ngx, L), F32),
-        vm((ngx, ngy * CAP + meta, L), F32),
-        vm((ngx, ngy * CAP + meta, L), F32),
+        vm((ngy, 2, ngx // 2 * (CAP + 1), L), F32),
+        vm((ngy, 2, ngx // 2 * (CAP + 1), L), F32),
+        vm((ngx, ngy * CAP + 1, L), F32),
+        vm((ngx, ngy * CAP + 1, L), F32),
         vm((slots, L), F32),
         vm((slots, L), F32),
         vm((cx * cz, slots), BF16),
@@ -841,8 +861,8 @@
         dma((STEPS, 26)),
         dma((26,)),
         dma((26,)),
-        dma((ngy + 1,)),
-        dma((ngy + 1,)),
+        dma((2 * ngy - 1,)),
+        dma((2 * ngy - 1,)),
         dma((2 * STEPS,)),
         dma((2 * STEPS,)),
     ]

time: 88.3 us -> 87.5 us (level); the launches traced: 88.2 us -> 86.5 us
  Pallas kernels: 86.7 us -> 85 us
    pallas_call x1, Pallas kernels: 84.4 us -> 82.7 us  [body(): pl.pallas_call(functools.partial(kernel, (ngx, ngy, ngz, cx, cz)), out_sh...]
where the time goes in v4:
time: 87.5 us; the launch traced here: 86.5 us
  Pallas kernels  85 us (97%)
  between operations  1.45 us (2%)
    pallas_call x1, Pallas kernels, body(): pl.pallas_call(functools.partial(kernel, (ngx, ngy, ngz, cx, cz)), out_sh...  82.7 us
    pallas_call x1, Pallas kernels, body(): pl.pallas_call(deliver, out_shape=(jax.ShapeDtypeStruct(velocity.shape, F...  2.29 us

profile of v4, /device:TPU:1, one launch (start us, length us, event | category | flops | bytes accessed | tf_op | source)
XLA Modules:
  0.0 86.5 jit_solution(17796742288987274730)
XLA Ops:
  1.3 82.7 %shard_map.113 = (f32[3,16,48,128]{3,2,1,0:T(8,128)}, f32[16,48,128]{2,1,0:T(8,128)}) custom-call(f32[3,16,48,128]{3,2,1,0:T(8,128)} %vel.1, f32[16,48,128]{2,1,0:T(8,128)} %prs.1, f32[256,128]{1,0:T(8,128)} %kern_h.1, s32[1,256]{1,0:T(1,128)} %bitcast.8, s32[1,256]{1,0:T(1,128)} %bitcast.9, s32[1,256]{1,0:T(1,128)} %bitcast.10, s32[1,1]{1,0:T(1,128)} %bitcast.7.cnt_h, ...), custom_call_target="tpu_custom_call" | custom-call | tf_op jit(solution)/shard_map/pallas_call | solution.py:869
  84.0 2.3 %shard_map.114 = (f32[3,16,48,128]{3,2,1,0:T(8,128)}, f32[16,48,128]{2,1,0:T(8,128)}) custom-call(f32[3,16,48,128]{3,2,1,0:T(8,128)} %get-tuple-element.4.vel, f32[16,48,128]{2,1,0:T(8,128)} %get-tuple-element.5.prs), custom_call_target="tpu_custom_call" | custom-call | tf_op jit(solution)/shard_map/pallas_call | solution.py:893

commit v5 on v4

--- a/solution.py
+++ b/solution.py
@@ -739,8 +739,8 @@
         wait_faces(step, faces)
         if step == 0:
             row_second(1)
+        inflow_second(step)
         stars = star_faces(step)
-        inflow_second(step)
         sources(step, stars)
         deep = deep_copies(GS.at[step], D, gys, gyr.at[step], gs_send.at[step], gs_recv.at[step])
         for copy in deep:

time: 87.5 us -> 89.4 us (1.022)
  Pallas kernels: 85 us -> 87.8 us
    pallas_call x1, Pallas kernels: 82.7 us -> 85.5 us  [body(): pl.pallas_call(functools.partial(kernel, (ngx, ngy, ngz, cx, cz)), out_sh...]
where the time goes in v5:
time: 89.4 us; the launch traced here: 89.2 us
  Pallas kernels  87.8 us (98%)
  between operations  1.45 us (2%)
    pallas_call x1, Pallas kernels, body(): pl.pallas_call(functools.partial(kernel, (ngx, ngy, ngz, cx, cz)), out_sh...  85.5 us
    pallas_call x1, Pallas kernels, body(): pl.pallas_call(deliver, out_shape=(jax.ShapeDtypeStruct(velocity.shape, F...  2.29 us

profile of v5, /device:TPU:1, one launch (start us, length us, event | category | flops | bytes accessed | tf_op | source)
XLA Modules:
  0.0 89.2 jit_solution(4959981409134263516)
XLA Ops:
  1.3 85.5 %shard_map.113 = (f32[3,16,48,128]{3,2,1,0:T(8,128)}, f32[16,48,128]{2,1,0:T(8,128)}) custom-call(f32[3,16,48,128]{3,2,1,0:T(8,128)} %vel.1, f32[16,48,128]{2,1,0:T(8,128)} %prs.1, f32[256,128]{1,0:T(8,128)} %kern_h.1, s32[1,256]{1,0:T(1,128)} %bitcast.8, s32[1,256]{1,0:T(1,128)} %bitcast.9, s32[1,256]{1,0:T(1,128)} %bitcast.10, s32[1,1]{1,0:T(1,128)} %bitcast.7.cnt_h, ...), custom_call_target="tpu_custom_call" | custom-call | tf_op jit(solution)/shard_map/pallas_call | solution.py:869
  86.8 2.3 %shard_map.114 = (f32[3,16,48,128]{3,2,1,0:T(8,128)}, f32[16,48,128]{2,1,0:T(8,128)}) custom-call(f32[3,16,48,128]{3,2,1,0:T(8,128)} %get-tuple-element.4.vel, f32[16,48,128]{2,1,0:T(8,128)} %get-tuple-element.5.prs), custom_call_target="tpu_custom_call" | custom-call | tf_op jit(solution)/shard_map/pallas_call | solution.py:893

commit v6 on v4

--- a/solution.py
+++ b/solution.py
@@ -502,7 +502,7 @@
     def forces(step):
         size = magnitudes(step)
 
-        @pl.loop(0, NGX, unroll=4)
+        @pl.loop(0, NGX, unroll=8)
         def _(g):
             at = pl.ds(pl.multiple_of(g * CAP * NGY, CAP * NGY), CAP * NGY)
             hot = jnp.where(TC[at, :] == lanes((CAP * NGY, L)).astype(F32), size, 0.0)
@@ -585,7 +585,7 @@
         unpack(fyr, 0, BF, 1)
         scales = weights()
 
-        @pl.loop(0, X, unroll=4)
+        @pl.loop(0, X, unroll=8)
         def _(x):
             plus = jnp.where(inside(x + 1), -0.2, 0.0)
             minus = jnp.where(inside(x - 1), -0.2, 0.0)
@@ -626,7 +626,7 @@
         at = pl.ds(D + 8, CZ)
         last = (SWEEPS + 1) % 2
 
-        @pl.loop(0, CX, unroll=4)
+        @pl.loop(0, CX, unroll=8)
         def _(x):
             deep = D + x + 1
             (left, right), _ = ring_sides(PR[last, 0, deep, at, :], PR[last, 1, deep, at, :])
@@ -684,7 +684,7 @@
         one_wait(whole, whole, row_send.at[row_all], row_recv.at[row_all], line_peer(1))
         which = lanes((CAP, L)) - rows_of((CAP, L))
 
-        @pl.loop(0, NGX, unroll=4)
+        @pl.loop(0, NGX, unroll=8)
         def _(g):
             for k in range(NGY):
                 row = R2[g, NGY * CAP : NGY * CAP + 1, :]

time: 87.5 us -> 87.1 us (level)
  no operation moved by 1% of the time
where the time goes in v6:
time: 87.1 us; the launch traced here: 86.1 us
  Pallas kernels  84.7 us (97%)
  between operations  1.45 us (2%)
    pallas_call x1, Pallas kernels, body(): pl.pallas_call(functools.partial(kernel, (ngx, ngy, ngz, cx, cz)), out_sh...  82.4 us
    pallas_call x1, Pallas kernels, body(): pl.pallas_call(deliver, out_shape=(jax.ShapeDtypeStruct(velocity.shape, F...  2.29 us

profile of v6, /device:TPU:1, one launch (start us, length us, event | category | flops | bytes accessed | tf_op | source)
XLA Modules:
  0.0 86.1 jit_solution(6423148454586962988)
XLA Ops:
  1.3 82.4 %shard_map.113 = (f32[3,16,48,128]{3,2,1,0:T(8,128)}, f32[16,48,128]{2,1,0:T(8,128)}) custom-call(f32[3,16,48,128]{3,2,1,0:T(8,128)} %vel.1, f32[16,48,128]{2,1,0:T(8,128)} %prs.1, f32[256,128]{1,0:T(8,128)} %kern_h.1, s32[1,256]{1,0:T(1,128)} %bitcast.8, s32[1,256]{1,0:T(1,128)} %bitcast.9, s32[1,256]{1,0:T(1,128)} %bitcast.10, s32[1,1]{1,0:T(1,128)} %bitcast.7.cnt_h, ...), custom_call_target="tpu_custom_call" | custom-call | tf_op jit(solution)/shard_map/pallas_call | solution.py:869
  83.7 2.3 %shard_map.114 = (f32[3,16,48,128]{3,2,1,0:T(8,128)}, f32[16,48,128]{2,1,0:T(8,128)}) custom-call(f32[3,16,48,128]{3,2,1,0:T(8,128)} %get-tuple-element.4.vel, f32[16,48,128]{2,1,0:T(8,128)} %get-tuple-element.5.prs), custom_call_target="tpu_custom_call" | custom-call | tf_op jit(solution)/shard_map/pallas_call | solution.py:893
